TPU v7x, 128 devices: a whole 4x4x4 slice. The times are simulated.
128 devices in a mesh: dp: 4 (over y_lo, core), seq: 32 (over x, y_hi, z).
Axes of the slice: x: 4, y: 4 (y_hi: 2, y_lo: 2; y = y_hi * 2 + y_lo), z: 4, core: 2. Of those that a mesh axis runs over, the one named last changes fastest.
Arguments:
- siblings: int32 [4, 64, 16], P('dp', 'seq'), may hold values from 0 to 63, all different within a row
- queries: bfloat16 [4, 64, 512, 2560], P('dp', 'seq'), may hold values from -6 to 6
- grad_out: bfloat16 [4, 64, 512, 2560], P('dp', 'seq'), may hold values from -6 to 6
- keys_in: bfloat16 [4, 64, 16, 512], P('dp', 'seq'), may hold values from -4 to 4
- input_values: bfloat16 [4, 64, 16, 512], P('dp', 'seq'), may hold values from -6 to 6
- summary: bfloat16 [4, 64, 16, 5120], P('dp', 'seq'), may hold values from -6 to 6
Outputs:
- query_gradient: bfloat16 [4, 64, 512, 2560], P('dp', 'seq')
- kv_weight_grad: float32 [5120, 1024], P(('dp', 'seq'))
Inputs may be any that keep to these rules, and one draw needn't show every extreme that they name: `siblings`: the 16 entries of one completion's list are distinct completions of the same prompt.
All inputs are finite; a program needn't handle non-finite values.
Results may differ from a plain program's by a relative error of at most 0.012.
Values may be sent and summed in bfloat16 or wider, within the bound.
A program may use at most 192 MiB of HBM per device.

v0:
```python
import math

import jax
import jax.numpy as jnp
from jax import lax
from jax.sharding import PartitionSpec as P

HEAD_SIZE = 128


def group_grads(query_tile_block, incoming_gradient, key_tile_block, value_tile_block, scaling):
    scores = (
        jnp.einsum(
            "ctrd,cld->crtl", query_tile_block, key_tile_block, preferred_element_type=jnp.float32
        )
        * scaling
    )
    largest = jnp.max(scores, axis=-1, keepdims=True)
    exponent = jnp.exp(scores - largest)
    probability = exponent / jnp.sum(exponent, axis=-1, keepdims=True)
    prob_half = probability.astype(jnp.bfloat16)
    attended = jnp.einsum(
        "crtl,cld->ctrd", prob_half, value_tile_block, preferred_element_type=jnp.float32
    )
    token_delta = jnp.sum(incoming_gradient * attended, axis=-1)
    row_delta = jnp.transpose(token_delta, (0, 2, 1))[..., None]
    prob_grad = jnp.einsum(
        "ctrd,cld->crtl", incoming_gradient, value_tile_block, preferred_element_type=jnp.float32
    )
    score_half = (probability * (prob_grad - row_delta)).astype(jnp.bfloat16)
    query_gradient = (
        jnp.einsum("crtl,cld->ctrd", score_half, key_tile_block, preferred_element_type=jnp.float32)
        * scaling
    )
    key_gradient = (
        jnp.einsum(
            "crtl,ctrd->cld", score_half, query_tile_block, preferred_element_type=jnp.float32
        )
        * scaling
    )
    value_gradient = jnp.einsum(
        "crtl,ctrd->cld", prob_half, incoming_gradient, preferred_element_type=jnp.float32
    )
    return (query_gradient, key_gradient, value_gradient)


def per_device(siblings, queries, grad_out, keys_in, input_values, summary):
    keys_all, values_all = (
        lax.all_gather(keys_in, "seq", axis=1, tiled=True),
        lax.all_gather(input_values, "seq", axis=1, tiled=True),
    )
    sibling = siblings[0]
    own_count, row_length = (queries.shape[1], queries.shape[2])
    everyone = keys_all.shape[1]
    neighbours, positions, key_value_width = (sibling.shape[1], keys_in.shape[2], keys_in.shape[3])
    kv_heads = key_value_width // HEAD_SIZE
    group_span = queries.shape[3] // kv_heads
    group_size = group_span // HEAD_SIZE
    scaling = 1.0 / math.sqrt(HEAD_SIZE)
    key_rows = keys_all[0][sibling].reshape(own_count, neighbours * positions, key_value_width)
    value_rows = values_all[0][sibling].reshape(own_count, neighbours * positions, key_value_width)
    query_parts, key_parts, value_parts = ([], [], [])
    for kv_head in range(kv_heads):
        query_tile_block = queries[
            0, :, :, kv_head * group_span : (kv_head + 1) * group_span
        ].reshape(own_count, row_length, group_size, HEAD_SIZE)
        incoming_gradient = grad_out[
            0, :, :, kv_head * group_span : (kv_head + 1) * group_span
        ].reshape(own_count, row_length, group_size, HEAD_SIZE)
        key_tile_block = key_rows[:, :, kv_head * HEAD_SIZE : (kv_head + 1) * HEAD_SIZE]
        value_tile_block = value_rows[:, :, kv_head * HEAD_SIZE : (kv_head + 1) * HEAD_SIZE]
        query_gradient, key_gradient, value_gradient = group_grads(
            query_tile_block, incoming_gradient, key_tile_block, value_tile_block, scaling
        )
        query_parts.append(query_gradient.reshape(own_count, row_length, group_span))
        key_parts.append(key_gradient)
        value_parts.append(value_gradient)
    query_out = jnp.concatenate(query_parts, axis=-1).astype(jnp.bfloat16)
    key_gradient = jnp.concatenate(key_parts, axis=-1).reshape(
        own_count * neighbours, positions * key_value_width
    )
    value_gradient = jnp.concatenate(value_parts, axis=-1).reshape(
        own_count * neighbours, positions * key_value_width
    )
    targets = sibling.reshape(-1)
    placing = (targets[:, None] == jnp.arange(everyone, dtype=jnp.int32)[None, :]).astype(
        jnp.float32
    )
    key_buffer = jnp.dot(placing.T, key_gradient, precision=lax.Precision.HIGHEST)
    value_buffer = jnp.dot(placing.T, value_gradient, precision=lax.Precision.HIGHEST)
    owner_keys, owner_values = (
        lax.psum_scatter(key_buffer, "seq", scatter_dimension=0, tiled=True),
        lax.psum_scatter(value_buffer, "seq", scatter_dimension=0, tiled=True),
    )
    grads_half = jnp.concatenate(
        [
            owner_keys.astype(jnp.bfloat16).reshape(own_count * positions, key_value_width),
            owner_values.astype(jnp.bfloat16).reshape(own_count * positions, key_value_width),
        ],
        axis=1,
    )
    hidden = summary[0].reshape(own_count * positions, summary.shape[3])
    weight_grad = lax.psum_scatter(
        jnp.einsum("sd,sk->dk", hidden, grads_half, preferred_element_type=jnp.float32),
        ("dp", "seq"),
        scatter_dimension=0,
        tiled=True,
    )
    return (query_out[None], weight_grad)


def solution(mesh):
    placed = (
        P("dp", "seq", None),
        P("dp", "seq", None, None),
        P("dp", "seq", None, None),
        P("dp", "seq", None, None),
        P("dp", "seq", None, None),
        P("dp", "seq", None, None),
    )
    return jax.shard_map(
        per_device,
        mesh=mesh,
        in_specs=placed,
        out_specs=(P("dp", "seq", None, None), P(("dp", "seq"), None)),
        check_vma=False,
    )
```

profile of v0, /device:TPU:1, one launch (start us, length us, event | category | flops | bytes accessed | tf_op | source)
XLA Modules:
  0.0 1172.4 jit_solution(1729174952819636855)
XLA Ops:
  7.2 0.7 all-gather.5.cloned.1.call-update
  8.0 0.7 all-gather.3.cloned.1.call-update
  8.7 0.8 eq.15
  9.5 0.7 compare_select_fusion
  10.2 4.6 fusion.72
  14.8 2.4 copy.211
  17.2 2.5 copy.215
  19.7 1.5 copy.213
  21.2 1.5 copy.217
  22.7 4.6 fusion.73
  27.2 0.6 copy.212
  27.9 1.6 copy.216
  29.5 2.4 copy.214
  32.0 2.4 copy.218
  35.6 43.3 %all-gather.5.cloned.1.call-done = bf16[1,64,16,512]{3,2,0,1:T(8,128)(2,1)} async-done(((bf16[1,2,16,512]{3,2,0,1:T(8,128)(2,1)}), bf16[1,64,16,512]{3,2,0,1:T(8,128)(2,1)}) %all-gather.5.cloned.1.call-update) | async-done | bytes 1048592 | tf_op jit(solution)/shard_map/all_gather | solution.py:50
  79.0 2.6 gather_fusion.1
  81.6 63.8 %all-gather.3.cloned.1.call-done = bf16[1,64,16,512]{3,2,0,1:T(8,128)(2,1)} async-done(((bf16[1,2,16,512]{3,2,0,1:T(8,128)(2,1)}), bf16[1,64,16,512]{3,2,0,1:T(8,128)(2,1)}) %all-gather.3.cloned.1.call-update) | async-done | bytes 1048592 | tf_op jit(solution)/shard_map/all_gather | solution.py:49
  145.4 1.8 gather_fusion
  147.2 5.6 fusion.74
  152.8 3.3 fusion.43
  156.1 1.7 convolution_bitcast_fusion.1
  157.8 2.1 fusion.32
  159.9 5.4 fusion.76
  165.3 3.3 fusion.41
  168.7 2.1 fusion.34
  170.8 1.7 convolution_bitcast_fusion.3
  172.5 5.4 fusion.75
  177.9 3.2 fusion.42
  181.1 2.1 fusion.33
  183.3 1.7 convolution_bitcast_fusion.2
  185.0 5.4 fusion.77
  190.3 3.5 fusion.40
  193.9 0.6 fusion.35
  194.5 1.0 convolution_bitcast_fusion.4
  195.8 3.5 fusion.5
  199.4 1.7 fusion.44
  201.7 0.8 fusion.13
  202.6 0.8 copy-done.17
  203.4 1.7 fusion.46
  205.1 0.9 fusion.9
  206.4 1.7 fusion.45
  208.2 1.3 copy.143
  209.5 1.4 reshape.134
  210.9 3.5 fusion.17
  214.4 1.5 copy-done.11
  215.9 1.0 fusion.47
  217.4 1.2 reshape.132
  218.6 2.3 fusion.64
  220.9 2.4 fusion.63
  223.3 186.3 %all-reduce.4 = (bf16[64,8192]{1,0:T(8,128)(2,1)S(1)}, bf16[64,8192]{1,0:T(8,128)(2,1)}) all-reduce(f32[64,8192]{1,0:T(8,128)} %fusion.63, f32[64,8192]{1,0:T(8,128)S(1)} %fusion.64), channel_id=3, replica_groups=mesh['dp'=4,'seq'=32] {'seq'}, use_global_device_ids=true, to_apply=%region_13.0.clone | all-reduce | flops 1048576 | bytes 6291456
  409.7 1.0 dynamic-slice_convert_fusion
  410.7 8.6 convolution_bitcast_fusion
  419.3 21.3 %copy.209 = f32[5120,1024]{1,0:T(8,128)} copy(f32[5120,1024]{0,1:T(8,128)} %convolution_bitcast_fusion) | data formatting | bytes 41943040
  440.7 1.7 copy-done.6
  442.5 1.6 multiply_convert_fusion
  444.1 2.6 copy.133
  446.7 1.6 multiply_convert_fusion.2
  448.4 2.6 copy.131
  450.9 1.6 multiply_convert_fusion.1
  452.6 2.6 copy.132
  455.2 1.6 multiply_convert_fusion.3
  456.8 2.6 copy.130
  459.5 4.6 pad_maximum_fusion
  464.0 701.8 %reduce-scatter.4.cloned.1.call-done = f32[40,1024]{1,0:T(8,128)} async-done(((f32[5120,1024]{1,0:T(8,128)}), f32[40,1024]{1,0:T(8,128)}) %reduce-scatter.4.cloned.1.call-update) | async-done | bytes 163856
  (95 shorter events, 3.0 us)
Async XLA Ops:
  7.2 403.5 %copy-start = (bf16[1,2,16,5120]{3,2,1,0:T(8,128)(2,1)S(1)}, bf16[1,2,16,5120]{3,2,1,0:T(8,128)(2,1)}, u32[]{:S(2)}) copy-start(bf16[1,2,16,5120]{3,2,1,0:T(8,128)(2,1)} %param.11) | copy-start | bytes 983044
  7.2 71.8 %all-gather.5.cloned.1.call-start = ((), (), s32[]{:S(2)}) async-start(), calls=%async_computation.2 | async-start | bytes 1081344 | tf_op jit(solution)/shard_map/all_gather | solution.py:50
  7.9 137.4 %all-gather.3.cloned.1.call-start = ((), (), s32[]{:S(2)}) async-start(), calls=%async_computation.1 | async-start | bytes 1081344 | tf_op jit(solution)/shard_map/all_gather | solution.py:49
  8.7 1157.2 %reduce-scatter.4.cloned.1.call-start = ((), (), s32[]{:S(2)}) async-start(), calls=%async_computation.3 | async-start | bytes 21135360
  29.5 4.9 copy-start.37
  147.2 37.8 %copy-start.19 = (bf16[32,16,512]{2,1,0:T(8,128)(2,1)}, bf16[32,16,512]{2,1,0:T(8,128)(2,1)S(1)}, u32[]{:S(2)}) copy-start(bf16[32,16,512]{2,1,0:T(8,128)(2,1)S(1)} %gather_fusion) | copy-start | bytes 1572868
  152.8 3.3 copy-start.28
  152.8 3.4 copy-start.3
  165.3 3.3 copy-start.30
  165.3 3.4 copy-start.1
  177.9 3.3 copy-start.32
  190.3 3.5 copy-start.21
  194.5 1.3 copy-start.4
  194.5 1.3 copy-start.29
  194.5 1.3 copy-start.34
  194.5 6.6 slice-start
  195.8 3.6 copy-start.18
  195.8 5.3 slice-start.1
  195.8 5.3 copy-start.31
  195.8 5.3 copy-start.35
  199.4 3.2 copy-start.5
  199.4 2.3 copy-start.2
  199.4 5.6 slice-start.2
  201.7 1.7 copy-start.17
  201.7 3.3 slice-start.3
  203.4 2.6 copy-start.7
  203.4 1.7 copy-start.33
  203.4 1.7 copy-start.36
  205.0 1.3 copy-start.16
  206.4 1.7 copy-start.9
  206.4 1.7 copy-start.22
  206.4 1.7 copy-start.23
  206.4 1.7 copy-start.24
  210.9 5.0 copy-start.15
  214.4 1.5 copy-start.11
  215.9 1.0 copy-start.25
  215.9 1.0 copy-start.26
  215.9 1.1 copy-start.27
  440.7 1.7 copy-start.6
  440.7 1.8 copy-start.20
  444.1 2.6 copy-start.8
  448.4 2.6 copy-start.10
  452.6 2.6 copy-start.12
  456.8 2.6 copy-start.13
  456.8 2.6 copy-start.14
Sparse Core Ops, SparseCore 0:
  11.0 67.9 all-gather.4
  81.9 63.3 all-gather.2
  440.8 725.0 reduce-scatter.3
where the time goes:
time: 1170 us
  waiting for transfers between devices  810 us (69%)
  blocking collectives  186 us (16%)
  local copies, waits for them, and re-layouts  72.6 us (6%)
  matrix products  69.4 us (6%)
  other arithmetic  18.8 us (2%)
  between operations  14.8 us (1%)
    unnamed x4, waiting for transfers between devices  703 us
    unnamed x1, blocking collectives  186 us
    all_gather x1, waiting for transfers between devices, per_device(): lax.all_gather(keys_in, 'seq', axis=1, tiled=True)  63.8 us
    all_gather x1, waiting for transfers between devices, per_device(): lax.all_gather(input_values, 'seq', axis=1, tiled=True)  43.3 us
    unnamed x94, local copies, waits for them, and re-layouts  42.5 us
  transfers between devices with their start and end apart: 3, of which 3 were waited for; matrix products, arithmetic and copies ran while one was open for 4% of the time, Pallas kernels for 0%

commit v1 on v0

v1 whole, which is shorter than its diff:
```python
import functools
import math

import jax
import jax.numpy as jnp
from jax import lax
from jax.experimental import pallas as pl
from jax.experimental.pallas import tpu as pltpu
from jax.sharding import PartitionSpec as P

HEAD = 128
MESH = pl.DeviceIdType.MESH
LIMIT = 56 * 1024 * 1024


def signal_peers(barrier, axis, me, count):
    def one(i, carry):
        pl.semaphore_signal(
            barrier,
            inc=1,
            device_id={axis: lax.rem(me + i, count)},
            device_id_type=MESH,
        )
        return carry

    lax.fori_loop(1, count, one, 0)


def wait_bytes(ref, count, sem):
    part = ref.at[pl.ds(0, count)]
    pltpu.make_async_copy(part, part, sem).wait()


def gather_kernel(
    n_seq, n_dp, k_ref, v_ref, s_ref, kv_out, s_out, kv_local, local_sem, send_sem, recv_sem
):
    me = lax.axis_index("seq")
    barrier = pltpu.get_barrier_semaphore()
    signal_peers(barrier, "seq", me, n_seq)
    groups = k_ref.shape[1] // HEAD
    for g in range(groups):
        kv_local[:, 2 * g * HEAD : (2 * g + 1) * HEAD] = k_ref[:, g * HEAD : (g + 1) * HEAD]
        kv_local[:, (2 * g + 1) * HEAD : (2 * g + 2) * HEAD] = v_ref[:, g * HEAD : (g + 1) * HEAD]
    pl.semaphore_wait(barrier, n_seq - 1)
    own_kv = pltpu.make_async_copy(kv_local, kv_out.at[me], local_sem.at[0])
    own_s = pltpu.make_async_copy(s_ref.at[me], s_out.at[me], local_sem.at[1])
    own_kv.start()
    own_s.start()

    def push(i, carry):
        peer = lax.rem(me + i, n_seq)
        pltpu.make_async_remote_copy(
            src_ref=kv_local,
            dst_ref=kv_out.at[me],
            send_sem=send_sem.at[0],
            recv_sem=recv_sem.at[0],
            device_id={"seq": peer},
            device_id_type=MESH,
        ).start()
        return carry

    lax.fori_loop(1, n_seq, push, 0)

    def push_summary(i, carry):
        peer = lax.rem(me + i, n_seq)
        pltpu.make_async_remote_copy(
            src_ref=s_ref.at[peer],
            dst_ref=s_out.at[me],
            send_sem=send_sem.at[1],
            recv_sem=recv_sem.at[1],
            device_id={"seq": peer},
            device_id_type=MESH,
        ).start()
        return carry

    lax.fori_loop(1, n_seq, push_summary, 0)
    own_kv.wait()
    own_s.wait()
    wait_bytes(kv_out, n_seq - 1, recv_sem.at[0])
    wait_bytes(s_out, n_seq - 1, recv_sem.at[1])
    wait_bytes(kv_out, n_seq - 1, send_sem.at[0])
    wait_bytes(s_out, n_seq - 1, send_sem.at[1])


def attention_kernel(
    siblings, q_ref, do_ref, kv_ref, dq_ref, part_ref, k_rows, v_rows, dk_acc, dv_acc, acc
):
    own = pl.program_id(1)
    span = kv_ref.shape[1]
    listed = k_rows.shape[0] // span
    heads = q_ref.shape[3] // HEAD
    scale = 1.0 / math.sqrt(HEAD)
    power = scale * math.log2(math.e)
    for j in range(listed):
        s = siblings[own * listed + j]
        k_rows[j * span : (j + 1) * span, :] = kv_ref[s, :, :HEAD]
        v_rows[j * span : (j + 1) * span, :] = kv_ref[s, :, HEAD:]
    keys = k_rows[...]
    values = v_rows[...]
    keys_t = keys.T
    for r in range(heads):
        cols = slice(r * HEAD, (r + 1) * HEAD)
        q = q_ref[0, 0, :, cols]
        do = do_ref[0, 0, :, cols]
        across = (((1,), (1,)), ((), ()))
        scores = lax.dot_general(keys, q, across, preferred_element_type=jnp.float32)
        prob_grad = lax.dot_general(values, do, across, preferred_element_type=jnp.float32)
        largest = jnp.max(scores, axis=0, keepdims=True)
        exponent = jnp.exp2((scores - largest) * power)
        prob = exponent * (1.0 / jnp.sum(exponent, axis=0, keepdims=True))
        prob_half = prob.astype(jnp.bfloat16)
        delta = jnp.sum(prob * prob_grad, axis=0, keepdims=True)
        score_half = (prob * (prob_grad - delta)).astype(jnp.bfloat16)
        dv = jnp.dot(prob_half, do, preferred_element_type=jnp.float32)
        dk = jnp.dot(score_half, q, preferred_element_type=jnp.float32)
        dq_t = jnp.dot(keys_t, score_half, preferred_element_type=jnp.float32)
        dq_ref[0, 0, :, cols] = (dq_t * scale).astype(jnp.bfloat16).T
        if r == 0:
            dk_acc[...] = dk
            dv_acc[...] = dv
        else:
            dk_acc[...] += dk
            dv_acc[...] += dv

    @pl.when(own == 0)
    def _():
        acc[...] = jnp.zeros_like(acc)

    for j in range(listed):
        s = siblings[own * listed + j]
        acc[s, :, :HEAD] += dk_acc[j * span : (j + 1) * span, :] * scale
        acc[s, :, HEAD:] += dv_acc[j * span : (j + 1) * span, :]

    @pl.when(own == pl.num_programs(1) - 1)
    def _():
        part_ref[...] = acc[...].astype(jnp.bfloat16)


def weight_kernel(
    n_seq,
    n_dp,
    part_ref,
    s_ref,
    out_ref,
    terms,
    own_half,
    halves,
    product,
    shares,
    send_sem,
    recv_sem,
    local_sem,
):
    me = lax.axis_index("seq")
    me_dp = lax.axis_index("dp")
    barrier = pltpu.get_barrier_semaphore()
    signal_peers(barrier, "seq", me, n_seq)
    signal_peers(barrier, "dp", me_dp, n_dp)
    pl.semaphore_wait(barrier, n_seq + n_dp - 2)
    own = pltpu.make_async_copy(part_ref.at[me], terms.at[me], local_sem.at[0])
    own.start()

    def push_terms(i, carry):
        peer = lax.rem(me + i, n_seq)
        pltpu.make_async_remote_copy(
            src_ref=part_ref.at[peer],
            dst_ref=terms.at[me],
            send_sem=send_sem.at[0],
            recv_sem=recv_sem.at[0],
            device_id={"seq": peer},
            device_id_type=MESH,
        ).start()
        return carry

    lax.fori_loop(1, n_seq, push_terms, 0)
    own.wait()
    wait_bytes(terms, n_seq - 1, recv_sem.at[0])

    def add(i, total):
        return total + terms[i].astype(jnp.float32)

    total = lax.fori_loop(1, n_seq, add, terms[0].astype(jnp.float32))
    own_half[...] = total.astype(jnp.bfloat16)
    own = pltpu.make_async_copy(own_half, halves.at[me], local_sem.at[0])
    own.start()

    def push_half(i, carry):
        peer = lax.rem(me + i, n_seq)
        pltpu.make_async_remote_copy(
            src_ref=own_half,
            dst_ref=halves.at[me],
            send_sem=send_sem.at[1],
            recv_sem=recv_sem.at[1],
            device_id={"seq": peer},
            device_id_type=MESH,
        ).start()
        return carry

    lax.fori_loop(1, n_seq, push_half, 0)
    own.wait()
    wait_bytes(halves, n_seq - 1, recv_sem.at[1])
    rows = n_seq * halves.shape[1]
    hidden = s_ref[...].reshape(rows, s_ref.shape[2])
    grads = halves[...].reshape(rows, halves.shape[2])
    product[...] = lax.dot_general(
        hidden, grads, (((0,), (0,)), ((), ())), preferred_element_type=jnp.float32
    ).reshape(product.shape)

    def push_share(i, carry):
        peer = lax.rem(me_dp + i, n_dp)
        pltpu.make_async_remote_copy(
            src_ref=product.at[peer],
            dst_ref=shares.at[me_dp],
            send_sem=send_sem.at[2],
            recv_sem=recv_sem.at[2],
            device_id={"dp": peer},
            device_id_type=MESH,
        ).start()
        return carry

    lax.fori_loop(1, n_dp, push_share, 0)
    own = pltpu.make_async_copy(product.at[me_dp], shares.at[me_dp], local_sem.at[0])
    own.start()
    own.wait()
    wait_bytes(shares, n_dp - 1, recv_sem.at[2])
    result = shares[0]
    for d in range(1, n_dp):
        result = result + shares[d]
    half = out_ref.shape[1] // 2
    for g in range(half // HEAD):
        out_ref[:, g * HEAD : (g + 1) * HEAD] = result[:, 2 * g * HEAD : (2 * g + 1) * HEAD]
        out_ref[:, half + g * HEAD : half + (g + 1) * HEAD] = result[
            :, (2 * g + 1) * HEAD : (2 * g + 2) * HEAD
        ]
    wait_bytes(terms, n_seq - 1, send_sem.at[0])
    wait_bytes(halves, n_seq - 1, send_sem.at[1])
    wait_bytes(shares, n_dp - 1, send_sem.at[2])


def per_device(n_dp, n_seq, siblings, queries, grad_out, keys_in, input_values, summary):
    _, own, tokens, q_width = queries.shape
    span, kv_width = keys_in.shape[2], keys_in.shape[3]
    listed = siblings.shape[2]
    groups = kv_width // HEAD
    rows = own * span
    everyone = n_seq * own
    width = summary.shape[3]
    block = width // (n_dp * n_seq)
    any_space = pl.BlockSpec(memory_space=pl.ANY)
    vmem = pl.BlockSpec(memory_space=pltpu.VMEM)
    pieces = (
        summary.reshape(rows, n_dp, n_seq, block)
        .transpose(2, 0, 1, 3)
        .reshape(n_seq, rows, n_dp * block)
    )
    kv_all, hidden = pl.pallas_call(
        functools.partial(gather_kernel, n_seq, n_dp),
        out_shape=(
            jax.ShapeDtypeStruct((n_seq, rows, 2 * kv_width), jnp.bfloat16),
            jax.ShapeDtypeStruct((n_seq, rows, n_dp * block), jnp.bfloat16),
        ),
        in_specs=[vmem, vmem, any_space],
        out_specs=(any_space, any_space),
        scratch_shapes=[
            pltpu.VMEM((rows, 2 * kv_width), jnp.bfloat16),
            pltpu.SemaphoreType.DMA((2,)),
            pltpu.SemaphoreType.DMA((2,)),
            pltpu.SemaphoreType.DMA((2,)),
        ],
        compiler_params=pltpu.CompilerParams(
            collective_id=0, has_side_effects=True, vmem_limit_bytes=LIMIT
        ),
    )(keys_in.reshape(rows, kv_width), input_values.reshape(rows, kv_width), pieces)
    kv_all = kv_all.reshape(everyone, span, 2 * kv_width)
    q_block = q_width // groups
    token_spec = pl.BlockSpec((1, 1, tokens, q_block), lambda g, c, s: (0, c, 0, g))
    dq, part = pl.pallas_call(
        attention_kernel,
        grid_spec=pltpu.PrefetchScalarGridSpec(
            num_scalar_prefetch=1,
            grid=(groups, own),
            in_specs=[
                token_spec,
                token_spec,
                pl.BlockSpec((everyone, span, 2 * HEAD), lambda g, c, s: (0, 0, g)),
            ],
            out_specs=[
                token_spec,
                pl.BlockSpec((everyone, span, 2 * HEAD), lambda g, c, s: (0, 0, g)),
            ],
            scratch_shapes=[
                pltpu.VMEM((listed * span, HEAD), jnp.bfloat16),
                pltpu.VMEM((listed * span, HEAD), jnp.bfloat16),
                pltpu.VMEM((listed * span, HEAD), jnp.float32),
                pltpu.VMEM((listed * span, HEAD), jnp.float32),
                pltpu.VMEM((everyone, span, 2 * HEAD), jnp.float32),
            ],
        ),
        out_shape=(
            jax.ShapeDtypeStruct(queries.shape, jnp.bfloat16),
            jax.ShapeDtypeStruct((everyone, span, 2 * kv_width), jnp.bfloat16),
        ),
        compiler_params=pltpu.CompilerParams(vmem_limit_bytes=LIMIT),
    )(siblings.reshape(-1), queries, grad_out, kv_all)
    weight_grad = pl.pallas_call(
        functools.partial(weight_kernel, n_seq, n_dp),
        out_shape=jax.ShapeDtypeStruct((block, 2 * kv_width), jnp.float32),
        in_specs=[any_space, vmem],
        out_specs=vmem,
        scratch_shapes=[
            pltpu.VMEM((n_seq, rows, 2 * kv_width), jnp.bfloat16),
            pltpu.VMEM((rows, 2 * kv_width), jnp.bfloat16),
            pltpu.VMEM((n_seq, rows, 2 * kv_width), jnp.bfloat16),
            pltpu.VMEM((n_dp, block, 2 * kv_width), jnp.float32),
            pltpu.VMEM((n_dp, block, 2 * kv_width), jnp.float32),
            pltpu.SemaphoreType.DMA((3,)),
            pltpu.SemaphoreType.DMA((3,)),
            pltpu.SemaphoreType.DMA((1,)),
        ],
        compiler_params=pltpu.CompilerParams(
            collective_id=1, has_side_effects=True, vmem_limit_bytes=LIMIT
        ),
    )(part.reshape(n_seq, rows, 2 * kv_width), hidden)
    return (dq, weight_grad)


def solution(mesh):
    placed = (
        P("dp", "seq", None),
        P("dp", "seq", None, None),
        P("dp", "seq", None, None),
        P("dp", "seq", None, None),
        P("dp", "seq", None, None),
        P("dp", "seq", None, None),
    )
    return jax.shard_map(
        functools.partial(per_device, mesh.shape["dp"], mesh.shape["seq"]),
        mesh=mesh,
        in_specs=placed,
        out_specs=(P("dp", "seq", None, None), P(("dp", "seq"), None)),
        check_vma=False,
    )
```

time: 1170 us -> 176 us (0.15)
  the two profiles are of different devices: /device:TPU:1 before, /device:TPU:25 now
where the time goes in v1:
time: 176 us; the launch traced here: 175 us
  Pallas kernels  167 us (95%)
  local copies, waits for them, and re-layouts  7.69 us (4%)
    pallas_call x1, Pallas kernels, per_device(): pl.pallas_call(functools.partial(weight_kernel, n_seq, n_dp), out_shape=j...  90.3 us
    pallas_call x1, Pallas kernels, per_device(): pl.pallas_call(functools.partial(gather_kernel, n_seq, n_dp), out_shape=(...  48.6 us
    pallas_call x1, Pallas kernels, per_device(): pl.pallas_call(attention_kernel, grid_spec=pltpu.PrefetchScalarGridSpec(n...  28 us

profile of v1, /device:TPU:25, one launch (start us, length us, event | category | flops | bytes accessed | tf_op | source)
XLA Modules:
  0.0 175.3 jit_solution(15674185342718239086)
XLA Ops:
  0.6 1.3 reshape.25.siblings
  1.9 2.9 %reshape.28 = bf16[32,4,32,40]{3,2,1,0:T(8,128)(2,1)S(1)} reshape(bf16[1,2,16,5120]{3,2,1,0:T(8,128)(2,1)} %param.11) | data formatting | bytes 655360 | tf_op jit(solution)/shard_map/reshape | solution.py:252
  4.8 0.5 copy.10
  5.4 1.4 reshape.29.s_ref
  6.7 48.6 %shard_map.77 = (bf16[32,32,1024]{2,1,0:T(8,128)(2,1)}, bf16[32,32,160]{2,1,0:T(8,128)(2,1)}) custom-call(bf16[32,512]{1,0:T(8,128)(2,1)} %bitcast.12, bf16[32,512]{1,0:T(8,128)(2,1)} %bitcast.13, bf16[32,32,160]{2,1,0:T(8,128)(2,1)} %reshape.29.s_ref), custom_call_target="tpu_custom_call" | custom-call | tf_op jit(solution)/shard_map/pallas_call | solution.py:256
  55.4 28.0 %shard_map.78 = (bf16[1,2,512,2560]{3,2,1,0:T(8,128)(2,1)}, bf16[64,16,1024]{2,1,0:T(8,128)(2,1)}) custom-call(s32[32]{0:T(128)} %reshape.25.siblings, bf16[1,2,512,2560]{3,2,1,0:T(8,128)(2,1)} %q_ref.1, bf16[1,2,512,2560]{3,2,1,0:T(8,128)(2,1)} %do_ref.1, bf16[64,16,1024]{2,1,0:T(8,128)(2,1)} %bitcast.10), custom_call_target="tpu_custom_call" | custom-call | tf_op jit(solution)/shard_map/pallas_call | solution.py:277
  83.4 90.3 %shard_map.79 = f32[40,1024]{1,0:T(8,128)} custom-call(bf16[32,32,1024]{2,1,0:T(8,128)(2,1)} %bitcast.11, bf16[32,32,160]{2,1,0:T(8,128)(2,1)} %get-tuple-element.9.s_ref), custom_call_target="tpu_custom_call" | custom-call | tf_op jit(solution)/shard_map/pallas_call | solution.py:305
  173.7 1.6 copy.12

commit v2 on v1

v2 whole, which is shorter than its diff:
```python
import functools
import math

import jax
import jax.numpy as jnp
from jax import lax
from jax.experimental import pallas as pl
from jax.experimental.pallas import tpu as pltpu
from jax.sharding import PartitionSpec as P

HEAD = 128
MESH = pl.DeviceIdType.MESH
RING = 4
SPREAD = 5
REDUCE = 5
LIMIT = 56 * 1024 * 1024


def signal_peers(barrier, axis, me, count):
    def one(i, carry):
        pl.semaphore_signal(
            barrier,
            inc=1,
            device_id={axis: lax.rem(me + i, count)},
            device_id_type=MESH,
        )
        return carry

    lax.fori_loop(1, count, one, 0)


def wait_bytes(ref, count, sem):
    part = ref.at[pl.ds(0, count)]
    pltpu.make_async_copy(part, part, sem).wait()


def ring(at, shift):
    return lax.rem(at + shift + RING, RING)


def place():
    me = lax.axis_index("seq")
    return me // (2 * RING), lax.rem(me // RING, 2), lax.rem(me, RING)


def peer_id(x, y, z):
    return {"seq": (x * 2 + y) * RING + z}


def neighbours():
    x, y, z = place()
    return [
        peer_id(x, 1 - y, z),
        peer_id(ring(x, 1), y, z),
        peer_id(ring(x, -1), y, z),
        peer_id(x, y, ring(z, 1)),
        peer_id(x, y, ring(z, -1)),
    ]


def remote(src, dst, peer, send_sem, recv_sem):
    return pltpu.make_async_remote_copy(
        src_ref=src,
        dst_ref=dst,
        send_sem=send_sem,
        recv_sem=recv_sem,
        device_id=peer,
        device_id_type=MESH,
    )


def spread_copies(buf, g, stage, send_sem, recv_sem):
    x, y, z = place()
    right, left = peer_id(ring(x, 1), y, z), peer_id(ring(x, -1), y, z)
    up, down = peer_id(x, y, ring(z, 1)), peer_id(x, y, ring(z, -1))
    every, both = pl.ds(0, RING), pl.ds(0, 2)
    xl, xr, zd, zu = ring(x, -1), ring(x, 1), ring(z, -1), ring(z, 1)
    moves = [
        [((x, y, z), peer_id(x, 1 - y, z))],
        [
            ((x, both, z, 0), up),
            ((x, both, z, 0), down),
            ((x, both, z, 1), right),
            ((x, both, z, 1), left),
        ],
        [
            ((x, 0, zd, 0), up),
            ((x, 1, zu, 0), down),
            ((xl, 0, z, 1), right),
            ((xr, 1, z, 1), left),
        ],
        [
            ((x, both, every, 0), right),
            ((x, both, every, 0), left),
            ((every, both, z, 1), up),
            ((every, both, z, 1), down),
        ],
        [
            ((xl, 0, every, 0), right),
            ((xr, 1, every, 0), left),
            ((every, 0, zd, 1), up),
            ((every, 1, zu, 1), down),
        ],
    ][stage]
    return [
        remote(
            buf.at[(g, *where)],
            buf.at[(g, *where)],
            peer,
            send_sem.at[g, 4 * stage + i],
            recv_sem.at[g, 4 * stage + i],
        )
        for i, (where, peer) in enumerate(moves)
    ]


def spread(buf, g, stage, send_sem, recv_sem):
    if stage > 0:
        for copy in spread_copies(buf, g, stage - 1, send_sem, recv_sem):
            copy.wait()
    if stage < SPREAD:
        for copy in spread_copies(buf, g, stage, send_sem, recv_sem):
            copy.start()


def reduce_copies(part, slots, g, stage, send_sem, recv_sem):
    x, y, z = place()
    right, left = peer_id(ring(x, 1), y, z), peer_id(ring(x, -1), y, z)
    up, down = peer_id(x, y, ring(z, 1)), peer_id(x, y, ring(z, -1))
    every, both = pl.ds(0, RING), pl.ds(0, 2)
    xl, xr, x2 = ring(x, -1), ring(x, 1), ring(x, 2)
    zd, zu, z2 = ring(z, -1), ring(z, 1), ring(z, 2)
    if stage == 4:
        moves = [((), peer_id(x, 1 - y, z))]
        source = slots[5]
    else:
        source = part
        moves = [
            [
                ((x2, 0, every, 0), right),
                ((x2, 1, every, 0), left),
                ((every, 0, z2, 1), up),
                ((every, 1, z2, 1), down),
            ],
            [
                ((xr, both, every, 0), right),
                ((xl, both, every, 0), left),
                ((every, both, zu, 1), up),
                ((every, both, zd, 1), down),
            ],
            [
                ((x, 0, z2, 0), up),
                ((x, 1, z2, 0), down),
                ((x2, 0, z, 1), right),
                ((x2, 1, z, 1), left),
            ],
            [
                ((x, both, zu, 0), up),
                ((x, both, zd, 0), down),
                ((xr, both, z, 1), right),
                ((xl, both, z, 1), left),
            ],
        ][stage]
    return [
        remote(
            source.at[(g, *where)],
            landing(slots, stage, i).at[g, i % 2 if stage == 1 else i],
            peer,
            send_sem.at[g, 4 * stage + i],
            recv_sem.at[g, 4 * stage + i],
        )
        for i, (where, peer) in enumerate(moves)
    ]


def landing(slots, stage, i):
    return slots[1][i // 2] if stage == 1 else slots[stage]


def wide(value):
    return value.astype(jnp.float32)


def reduce(part, slots, halves, g, stage, send_sem, recv_sem):
    x, y, z = place()
    every, both = slice(None), slice(None)
    xl, xr, zd, zu = ring(x, -1), ring(x, 1), ring(z, -1), ring(z, 1)
    if stage > 0:
        for copy in reduce_copies(part, slots, g, stage - 1, send_sem, recv_sem):
            copy.wait()
        came = slots[stage - 1]

        def add(where, i):
            at = (g, *where)
            part[at] = (wide(part[at]) + wide(came[g, i])).astype(part.dtype)

        def three(where, term):
            total = wide(part[(g, *where)]) + wide(term[g, 0]) + wide(term[g, 1])
            part[(g, *where)] = total.astype(part.dtype)

        if stage == 1:
            add((xr, 0, every, 0), 0)
            add((xl, 1, every, 0), 1)
            add((every, 0, zu, 1), 2)
            add((every, 1, zd, 1), 3)
        elif stage == 2:
            three((x, both, every, 0), came[0])
            three((every, both, z, 1), came[1])
        elif stage == 3:
            add((x, 0, zu, 0), 0)
            add((x, 1, zd, 0), 1)
            add((xr, 0, z, 1), 2)
            add((xl, 1, z, 1), 3)
        elif stage == 4:
            for half, first in ((0, 0), (1, 2)):
                for at, total in ((1 - y, slots[5]), (y, slots[6])):
                    total[g, half] = (
                        wide(part[g, x, at, z, half])
                        + wide(came[g, first, at])
                        + wide(came[g, first + 1, at])
                    )
        else:
            halves[g, x, y, z] = (slots[6][g] + came[g, 0]).astype(halves.dtype)
    if stage < REDUCE:
        for copy in reduce_copies(part, slots, g, stage, send_sem, recv_sem):
            copy.start()


def reduce_slots(groups, span, wide_cols, kind):
    row = (span, wide_cols)
    return [
        pltpu.VMEM((groups, 4, RING, *row), kind),
        pltpu.VMEM((groups, 2, 2, RING, *row), kind),
        pltpu.VMEM((groups, 2, RING, 2, *row), kind),
        pltpu.VMEM((groups, 4, *row), kind),
        pltpu.VMEM((groups, 4, 2, *row), kind),
        pltpu.VMEM((groups, 1, 2, *row), jnp.float32),
        pltpu.VMEM((groups, 2, *row), jnp.float32),
        pltpu.VMEM((groups, 2, *row), jnp.float32),
    ]


def wavefront(groups, stages, step):
    for d in range(groups + stages):
        for g in range(groups):
            if 0 <= d - g <= stages:
                step(g, d - g)


def gather_kernel(
    n_seq, k_ref, v_ref, s_ref, kv_out, s_out, kv, local_sem, send_sem, recv_sem, s_send, s_recv
):
    me = lax.axis_index("seq")
    x, y, z = place()
    barrier = pltpu.get_barrier_semaphore()
    signal_peers(barrier, "seq", me, n_seq)
    groups = k_ref.shape[2] // HEAD
    for g in range(groups):
        cols = slice(g * HEAD, (g + 1) * HEAD)
        kv[g, x, y, z, :, :, :HEAD] = k_ref[:, :, cols]
        kv[g, x, y, z, :, :, HEAD:] = v_ref[:, :, cols]
    pl.semaphore_wait(barrier, n_seq - 1)
    for g in range(groups):
        spread(kv, g, 0, send_sem, recv_sem)
    own_s = pltpu.make_async_copy(s_ref.at[me], s_out.at[me], local_sem.at[0])
    own_s.start()

    def push_summary(i, carry):
        peer = lax.rem(me + i, n_seq)
        remote(
            s_ref.at[peer], s_out.at[me], {"seq": peer}, s_send.at[0], s_recv.at[0]
        ).start()
        return carry

    lax.fori_loop(1, n_seq, push_summary, 0)
    wavefront(
        groups, SPREAD - 1, lambda g, stage: spread(kv, g, stage + 1, send_sem, recv_sem)
    )
    done = pltpu.make_async_copy(kv, kv_out, local_sem.at[1])
    done.start()
    own_s.wait()
    wait_bytes(s_out, n_seq - 1, s_recv.at[0])
    wait_bytes(s_out, n_seq - 1, s_send.at[0])
    done.wait()


def attention_kernel(
    siblings, q_ref, do_ref, kv_ref, dq_ref, part_ref, k_rows, v_rows, dk_acc, dv_acc, acc
):
    own = pl.program_id(1)
    span = kv_ref.shape[2]
    listed = k_rows.shape[0] // span
    heads = q_ref.shape[3] // HEAD
    scale = 1.0 / math.sqrt(HEAD)
    power = scale * math.log2(math.e)
    for j in range(listed):
        s = siblings[own * listed + j]
        k_rows[j * span : (j + 1) * span, :] = kv_ref[0, s, :, :HEAD]
        v_rows[j * span : (j + 1) * span, :] = kv_ref[0, s, :, HEAD:]
    keys = k_rows[...]
    values = v_rows[...]
    keys_t = keys.T
    for r in range(heads):
        cols = slice(r * HEAD, (r + 1) * HEAD)
        q = q_ref[0, 0, :, cols]
        do = do_ref[0, 0, :, cols]
        across = (((1,), (1,)), ((), ()))
        scores = lax.dot_general(keys, q, across, preferred_element_type=jnp.float32)
        prob_grad = lax.dot_general(values, do, across, preferred_element_type=jnp.float32)
        largest = jnp.max(scores, axis=0, keepdims=True)
        exponent = jnp.exp2((scores - largest) * power)
        prob = exponent * (1.0 / jnp.sum(exponent, axis=0, keepdims=True))
        prob_half = prob.astype(jnp.bfloat16)
        delta = jnp.sum(prob * prob_grad, axis=0, keepdims=True)
        score_half = (prob * (prob_grad - delta)).astype(jnp.bfloat16)
        dv = jnp.dot(prob_half, do, preferred_element_type=jnp.float32)
        dk = jnp.dot(score_half, q, preferred_element_type=jnp.float32)
        dq_t = jnp.dot(keys_t, score_half, preferred_element_type=jnp.float32)
        dq_ref[0, 0, :, cols] = (dq_t * scale).astype(jnp.bfloat16).T
        if r == 0:
            dk_acc[...] = dk
            dv_acc[...] = dv
        else:
            dk_acc[...] += dk
            dv_acc[...] += dv

    @pl.when(own == 0)
    def _():
        acc[...] = jnp.zeros_like(acc)

    for j in range(listed):
        s = siblings[own * listed + j]
        acc[s, :, :HEAD] += dk_acc[j * span : (j + 1) * span, :] * scale
        acc[s, :, HEAD:] += dv_acc[j * span : (j + 1) * span, :]

    @pl.when(own == pl.num_programs(1) - 1)
    def _():
        part_ref[0] = acc[...].astype(jnp.bfloat16)


def weight_kernel(
    groups,
    n_dp,
    part_ref,
    s_ref,
    out_ref,
    part,
    halves,
    product,
    shares,
    s0,
    s1a,
    s1b,
    s2,
    s3,
    s4,
    s5,
    s6,
    red_send,
    red_recv,
    spr_send,
    spr_recv,
    send_sem,
    recv_sem,
    local_sem,
):
    me_dp = lax.axis_index("dp")
    barrier = pltpu.get_barrier_semaphore()
    for peer in neighbours():
        pl.semaphore_signal(barrier, inc=1, device_id=peer, device_id_type=MESH)
    signal_peers(barrier, "dp", me_dp, n_dp)
    load = pltpu.make_async_copy(part_ref, part, local_sem.at[0])
    load.start()
    pl.semaphore_wait(barrier, 5 + n_dp - 1)
    load.wait()
    slots = (s0, (s1a, s1b), s2, s3, s4, s5, s6)

    def step(g, stage):
        if stage <= REDUCE:
            reduce(part, slots, halves, g, stage, red_send, red_recv)
        if stage >= REDUCE:
            spread(halves, g, stage - REDUCE, spr_send, spr_recv)

    wavefront(groups, REDUCE + SPREAD, step)
    rows = s_ref.shape[0] * s_ref.shape[1]
    hidden = s_ref[...].reshape(rows, s_ref.shape[2])
    for g in range(groups):
        grads = halves[g].reshape(rows, 2 * HEAD)
        got = lax.dot_general(
            hidden, grads, (((0,), (0,)), ((), ())), preferred_element_type=jnp.float32
        ).reshape(product.shape[0], product.shape[1], 2 * HEAD)
        product[:, :, g * HEAD : (g + 1) * HEAD] = got[:, :, :HEAD]
        product[:, :, (groups + g) * HEAD : (groups + g + 1) * HEAD] = got[:, :, HEAD:]

    def push_share(i, carry):
        peer = lax.rem(me_dp + i, n_dp)
        remote(
            product.at[peer], shares.at[me_dp], {"dp": peer}, send_sem.at[0], recv_sem.at[0]
        ).start()
        return carry

    lax.fori_loop(1, n_dp, push_share, 0)
    shares[me_dp] = product[me_dp]
    wait_bytes(shares, n_dp - 1, recv_sem.at[0])
    result = shares[0]
    for d in range(1, n_dp):
        result = result + shares[d]
    out_ref[...] = result
    wait_bytes(shares, n_dp - 1, send_sem.at[0])


def per_device(n_dp, n_seq, siblings, queries, grad_out, keys_in, input_values, summary):
    _, own, tokens, q_width = queries.shape
    span, kv_width = keys_in.shape[2], keys_in.shape[3]
    listed = siblings.shape[2]
    groups = kv_width // HEAD
    rows = own * span
    everyone = n_seq * own
    width = summary.shape[3]
    block = width // (n_dp * n_seq)
    any_space = pl.BlockSpec(memory_space=pl.ANY)
    vmem = pl.BlockSpec(memory_space=pltpu.VMEM)
    pieces = (
        summary.reshape(rows, n_dp, n_seq, block)
        .transpose(2, 0, 1, 3)
        .reshape(n_seq, rows, n_dp * block)
    )
    tile = (RING, 2, RING, own, span, 2 * HEAD)
    kv_all, hidden = pl.pallas_call(
        functools.partial(gather_kernel, n_seq),
        out_shape=(
            jax.ShapeDtypeStruct((groups, *tile), jnp.bfloat16),
            jax.ShapeDtypeStruct((n_seq, rows, n_dp * block), jnp.bfloat16),
        ),
        in_specs=[vmem, vmem, any_space],
        out_specs=(any_space, any_space),
        scratch_shapes=[
            pltpu.VMEM((groups, *tile), jnp.bfloat16),
            pltpu.SemaphoreType.DMA((2,)),
            pltpu.SemaphoreType.DMA((groups, 4 * SPREAD)),
            pltpu.SemaphoreType.DMA((groups, 4 * SPREAD)),
            pltpu.SemaphoreType.DMA((1,)),
            pltpu.SemaphoreType.DMA((1,)),
        ],
        compiler_params=pltpu.CompilerParams(
            collective_id=0, has_side_effects=True, vmem_limit_bytes=LIMIT
        ),
    )(keys_in[0], input_values[0], pieces)
    kv_all = kv_all.reshape(groups, everyone, span, 2 * HEAD)
    q_block = q_width // groups
    token_spec = pl.BlockSpec((1, 1, tokens, q_block), lambda g, c, s: (0, c, 0, g))
    dq, part = pl.pallas_call(
        attention_kernel,
        grid_spec=pltpu.PrefetchScalarGridSpec(
            num_scalar_prefetch=1,
            grid=(groups, own),
            in_specs=[
                token_spec,
                token_spec,
                pl.BlockSpec((1, everyone, span, 2 * HEAD), lambda g, c, s: (g, 0, 0, 0)),
            ],
            out_specs=[
                token_spec,
                pl.BlockSpec((1, everyone, span, 2 * HEAD), lambda g, c, s: (g, 0, 0, 0)),
            ],
            scratch_shapes=[
                pltpu.VMEM((listed * span, HEAD), jnp.bfloat16),
                pltpu.VMEM((listed * span, HEAD), jnp.bfloat16),
                pltpu.VMEM((listed * span, HEAD), jnp.float32),
                pltpu.VMEM((listed * span, HEAD), jnp.float32),
                pltpu.VMEM((everyone, span, 2 * HEAD), jnp.float32),
            ],
        ),
        out_shape=(
            jax.ShapeDtypeStruct(queries.shape, jnp.bfloat16),
            jax.ShapeDtypeStruct((groups, everyone, span, 2 * HEAD), jnp.bfloat16),
        ),
        compiler_params=pltpu.CompilerParams(vmem_limit_bytes=LIMIT),
    )(siblings.reshape(-1), queries, grad_out, kv_all)
    weight_grad = pl.pallas_call(
        functools.partial(weight_kernel, groups, n_dp),
        out_shape=jax.ShapeDtypeStruct((block, 2 * kv_width), jnp.float32),
        in_specs=[any_space, vmem],
        out_specs=vmem,
        scratch_shapes=[
            pltpu.VMEM((groups, *tile), jnp.bfloat16),
            pltpu.VMEM((groups, *tile), jnp.bfloat16),
            pltpu.VMEM((n_dp, block, 2 * kv_width), jnp.float32),
            pltpu.VMEM((n_dp, block, 2 * kv_width), jnp.float32),
            *reduce_slots(groups, span, 2 * HEAD, jnp.bfloat16),
            pltpu.SemaphoreType.DMA((groups, 4 * REDUCE)),
            pltpu.SemaphoreType.DMA((groups, 4 * REDUCE)),
            pltpu.SemaphoreType.DMA((groups, 4 * SPREAD)),
            pltpu.SemaphoreType.DMA((groups, 4 * SPREAD)),
            pltpu.SemaphoreType.DMA((1,)),
            pltpu.SemaphoreType.DMA((1,)),
            pltpu.SemaphoreType.DMA((1,)),
        ],
        compiler_params=pltpu.CompilerParams(
            collective_id=1, has_side_effects=True, vmem_limit_bytes=LIMIT
        ),
    )(part.reshape(groups, *tile), hidden)
    return (dq, weight_grad)


def solution(mesh):
    placed = (
        P("dp", "seq", None),
        P("dp", "seq", None, None),
        P("dp", "seq", None, None),
        P("dp", "seq", None, None),
        P("dp", "seq", None, None),
        P("dp", "seq", None, None),
    )
    return jax.shard_map(
        functools.partial(per_device, mesh.shape["dp"], mesh.shape["seq"]),
        mesh=mesh,
        in_specs=placed,
        out_specs=(P("dp", "seq", None, None), P(("dp", "seq"), None)),
        check_vma=False,
    )
```

time: 176 us -> 147 us (0.84)
  the two profiles are of different devices: /device:TPU:25 before, /device:TPU:1 now
where the time goes in v2:
time: 147 us
  Pallas kernels  139 us (95%)
  local copies, waits for them, and re-layouts  7.69 us (5%)
    pallas_call x1, Pallas kernels, per_device(): pl.pallas_call(functools.partial(weight_kernel, groups, n_dp), out_shape=...  68.6 us
    pallas_call x1, Pallas kernels, per_device(): pl.pallas_call(functools.partial(gather_kernel, n_seq), out_shape=(jax.Sh...  41.9 us
    pallas_call x1, Pallas kernels, per_device(): pl.pallas_call(attention_kernel, grid_spec=pltpu.PrefetchScalarGridSpec(n...  28.1 us
    reshape x2, local copies, waits for them, and re-layouts, per_device(): summary.reshape(rows, n_dp, n_seq, block).transpose(2, 0, 1, 3)  3.46 us

profile of v2, /device:TPU:1, one launch (start us, length us, event | category | flops | bytes accessed | tf_op | source)
XLA Modules:
  0.0 147.0 jit_solution(15648541380310550635)
XLA Ops:
  0.6 1.3 reshape.19.siblings
  1.9 2.9 %reshape.20 = bf16[32,4,32,40]{3,2,1,0:T(8,128)(2,1)S(1)} reshape(bf16[1,2,16,5120]{3,2,1,0:T(8,128)(2,1)} %param.11) | data formatting | bytes 655360 | tf_op jit(solution)/shard_map/reshape | solution.py:424
  4.8 0.5 copy.10
  5.4 1.4 reshape.21.s_ref
  6.7 41.9 %shard_map.77 = (bf16[4,4,2,4,2,16,256]{6,5,4,3,2,1,0:T(8,128)(2,1)}, bf16[32,32,160]{2,1,0:T(8,128)(2,1)}) custom-call(bf16[2,16,512]{2,1,0:T(8,128)(2,1)} %bitcast.12, bf16[2,16,512]{2,1,0:T(8,128)(2,1)} %bitcast.13, bf16[32,32,160]{2,1,0:T(8,128)(2,1)} %reshape.21.s_ref), custom_call_target="tpu_custom_call" | custom-call | tf_op jit(solution)/shard_map/pallas_call | solution.py:429
  48.7 28.1 %shard_map.78 = (bf16[1,2,512,2560]{3,2,1,0:T(8,128)(2,1)}, bf16[4,64,16,256]{3,2,1,0:T(8,128)(2,1)}) custom-call(s32[32]{0:T(128)} %reshape.19.siblings, bf16[1,2,512,2560]{3,2,1,0:T(8,128)(2,1)} %q_ref.1, bf16[1,2,512,2560]{3,2,1,0:T(8,128)(2,1)} %do_ref.1, bf16[4,64,16,256]{3,2,1,0:T(8,128)(2,1)} %bitcast.10), custom_call_target="tpu_custom_call" | custom-call | tf_op jit(solution)/shard_map/pallas_call | solution.py:452
  76.8 68.6 %shard_map.79 = f32[40,1024]{1,0:T(8,128)} custom-call(bf16[4,4,2,4,2,16,256]{6,5,4,3,2,1,0:T(8,128)(2,1)} %bitcast.11, bf16[32,32,160]{2,1,0:T(8,128)(2,1)} %get-tuple-element.9.s_ref), custom_call_target="tpu_custom_call" | custom-call | tf_op jit(solution)/shard_map/pallas_call | solution.py:480
  145.4 1.6 %copy.12 = f32[40,1024]{1,0:T(8,128)} copy(f32[40,1024]{1,0:T(8,128)} %shard_map.79) | data formatting | bytes 327680

commit v3 on v0

v3 whole, which is shorter than its diff:
```python
import functools
import math

import jax
import jax.numpy as jnp
from jax import lax
from jax.experimental import pallas as pl
from jax.experimental.pallas import tpu as pltpu
from jax.sharding import PartitionSpec as P

HEAD = 128
MESH = pl.DeviceIdType.MESH
LIMIT = 56 * 1024 * 1024
RING = 4
PLANE = 2 * RING


def signal_peers(barrier, axis, me, count):
    def one(i, carry):
        pl.semaphore_signal(
            barrier,
            inc=1,
            device_id={axis: lax.rem(me + i, count)},
            device_id_type=MESH,
        )
        return carry

    lax.fori_loop(1, count, one, 0)


def wait_blocks(ref, count, sem):
    part = ref.at[pl.ds(0, count)]
    pltpu.make_async_copy(part, part, sem).wait()


def wide(value):
    return value.astype(jnp.float32)


def ring(at, shift):
    return lax.rem(at + shift, RING)


def place():
    me = lax.axis_index("seq")
    return me // PLANE, lax.rem(me // RING, 2), lax.rem(me, RING)


def peer_id(x, y, z):
    return {"seq": x * PLANE + y * RING + z}


def remote(src, dst, peer, send_sem, recv_sem):
    return pltpu.make_async_remote_copy(
        src_ref=src,
        dst_ref=dst,
        send_sem=send_sem,
        recv_sem=recv_sem,
        device_id=peer,
        device_id_type=MESH,
    )


def plane_shifts():
    return [(i // RING, i % RING) for i in range(1, PLANE)]


class Spread:
    def __init__(self, buf, ruler, send_sem, recv_sem):
        self.buf, self.ruler = buf, ruler
        self.send_sem, self.recv_sem = send_sem, recv_sem

    def start_plane(self, g):
        x, y, z = place()
        for dy, shift in plane_shifts():
            other = lax.rem(y + dy, 2)
            for half, peer in (
                (0, peer_id(x, other, ring(z, shift))),
                (1, peer_id(ring(x, shift), other, z)),
            ):
                block = self.buf.at[g, x, y, z, half]
                remote(block, block, peer, self.send_sem.at[g, 0], self.recv_sem.at[g, 0]).start()

    def wait_plane(self, g):
        wait_blocks(self.ruler, 2 * (PLANE - 1), self.recv_sem.at[g, 0])

    def start_line(self, g):
        x, y, z = place()
        for shift in (1, 3, 2):
            first = self.buf.at[g, x, :, :, 0]
            second = self.buf.at[g, :, :, z, 1]
            sems = (self.send_sem.at[g, 1], self.recv_sem.at[g, 1])
            remote(first, first, peer_id(ring(x, shift), y, z), *sems).start()
            remote(second, second, peer_id(x, y, ring(z, shift)), *sems).start()

    def wait_line(self, g):
        wait_blocks(self.ruler, 2 * (RING - 1) * PLANE, self.recv_sem.at[g, 1])

    def wait_sent(self, g):
        wait_blocks(self.ruler, 2 * (PLANE - 1), self.send_sem.at[g, 0])
        wait_blocks(self.ruler, 2 * (RING - 1) * PLANE, self.send_sem.at[g, 1])


class Reduce:
    def __init__(self, part, line_a, line_b, sum_a, sum_b, plane, ruler, send_sem, recv_sem):
        self.part, self.ruler = part, ruler
        self.line_a, self.line_b = line_a, line_b
        self.sum_a, self.sum_b, self.plane = sum_a, sum_b, plane
        self.send_sem, self.recv_sem = send_sem, recv_sem

    def start_line(self, g):
        x, y, z = place()
        sems = (self.send_sem.at[g, 0], self.recv_sem.at[g, 0])
        for shift in (1, 3, 2):
            xs, zs = ring(x, shift), ring(z, shift)
            slot = shift - 1
            remote(
                self.part.at[g, xs, :, :, 0], self.line_a.at[g, slot], peer_id(xs, y, z), *sems
            ).start()
            remote(
                self.part.at[g, :, :, zs, 1], self.line_b.at[g, slot], peer_id(x, y, zs), *sems
            ).start()

    def line_to_plane(self, g):
        x, y, z = place()
        wait_blocks(self.ruler, 2 * (RING - 1) * PLANE, self.recv_sem.at[g, 0])
        total_a = wide(self.part[g, x, :, :, 0])
        total_b = wide(self.part[g, :, :, z, 1])
        for slot in range(RING - 1):
            total_a += wide(self.line_a[g, slot])
            total_b += wide(self.line_b[g, slot])
        self.sum_a[g] = total_a.astype(jnp.bfloat16)
        self.sum_b[g] = total_b.astype(jnp.bfloat16)
        sems = (self.send_sem.at[g, 1], self.recv_sem.at[g, 1])
        for i, (dy, shift) in enumerate(plane_shifts()):
            other, xs, zs = lax.rem(y + dy, 2), ring(x, shift), ring(z, shift)
            remote(
                self.sum_a.at[g, other, zs], self.plane.at[g, 0, i], peer_id(x, other, zs), *sems
            ).start()
            remote(
                self.sum_b.at[g, xs, other], self.plane.at[g, 1, i], peer_id(xs, other, z), *sems
            ).start()

    def finish(self, g, out):
        x, y, z = place()
        wait_blocks(self.ruler, 2 * (PLANE - 1), self.recv_sem.at[g, 1])
        for half, own in ((0, self.sum_a[g, y, z]), (1, self.sum_b[g, x, y])):
            total = wide(own)
            for i in range(PLANE - 1):
                total += wide(self.plane[g, half, i])
            out[g, x, y, z, half] = total.astype(out.dtype)

    def wait_sent(self, g):
        wait_blocks(self.ruler, 2 * (RING - 1) * PLANE, self.send_sem.at[g, 0])
        wait_blocks(self.ruler, 2 * (PLANE - 1), self.send_sem.at[g, 1])


def kernel(
    n_seq,
    n_dp,
    siblings,
    k_ref,
    v_ref,
    s_ref,
    q_hbm,
    do_hbm,
    dq_hbm,
    out_ref,
    q_all,
    do_all,
    dq_all,
    kv,
    kv_now,
    k_rows,
    v_rows,
    key_acc,
    value_acc,
    listed_grads,
    placing,
    part,
    line_a,
    line_b,
    sum_a,
    sum_b,
    plane,
    halves,
    hidden,
    hidden_t,
    product,
    shares,
    ruler,
    load_sem,
    store_sem,
    spread_send,
    spread_recv,
    reduce_send,
    reduce_recv,
    again_send,
    again_recv,
    share_send,
    share_recv,
    summary_send,
    summary_recv,
):
    me, me_dp = lax.axis_index("seq"), lax.axis_index("dp")
    x, y, z = place()
    groups, own, tokens, q_block = q_all.shape
    heads = q_block // HEAD
    span = k_ref.shape[1]
    listed = siblings.shape[2]
    reach = listed * span
    rows = n_seq * own * span
    scale = 1.0 / math.sqrt(HEAD)
    power = scale * math.log2(math.e)

    barrier = pltpu.get_barrier_semaphore()
    signal_peers(barrier, "seq", me, n_seq)
    signal_peers(barrier, "dp", me_dp, n_dp)
    loads = []
    for g in range(groups):
        cols = pl.ds(g * q_block, q_block)
        for c in range(own):
            loads.append(pltpu.make_async_copy(q_hbm.at[0, c, :, cols], q_all.at[g, c], load_sem.at[0, g, c]))
            loads.append(pltpu.make_async_copy(do_hbm.at[0, c, :, cols], do_all.at[g, c], load_sem.at[1, g, c]))
    for load in loads:
        load.start()
    for g in range(groups):
        cols = slice(g * HEAD, (g + 1) * HEAD)
        kv[g, x, y, z, :, :, :HEAD] = k_ref[:, :, cols]
        kv[g, x, y, z, :, :, HEAD:] = v_ref[:, :, cols]
    pl.semaphore_wait(barrier, n_seq + n_dp - 2)

    first = Spread(kv, ruler, spread_send, spread_recv)
    again = Spread(halves, ruler, again_send, again_recv)
    summing = Reduce(part, line_a, line_b, sum_a, sum_b, plane, ruler, reduce_send, reduce_recv)

    def over_groups(step):
        def one(g, carry):
            step(g)
            return carry

        lax.fori_loop(0, groups, one, 0)

    over_groups(first.start_plane)

    lane = lax.broadcasted_iota(jnp.int32, (1, own * reach), 1)
    target = lax.rem(lane, span)
    for c in range(own):
        for j in range(listed):
            here = lane // span == c * listed + j
            target += jnp.where(here, siblings[0, c, j] * span, 0)
    row = lax.broadcasted_iota(jnp.int32, (rows, own * reach), 0)
    placing[...] = jnp.where(row == target, 1.0, 0.0).astype(jnp.bfloat16)

    def line(g):
        first.wait_plane(g)
        first.start_line(g)

    over_groups(line)

    hidden[me] = s_ref[me]

    def push_summary(i, carry):
        peer = lax.rem(me + i, n_seq)
        remote(
            s_ref.at[peer], hidden.at[me], {"seq": peer}, summary_send.at[0], summary_recv.at[0]
        ).start()
        return carry

    lax.fori_loop(1, n_seq, push_summary, 0)
    for load in loads:
        load.wait()

    def attend(g, c, r):
        cols = slice(r * HEAD, (r + 1) * HEAD)
        keys, values = k_rows[...], v_rows[...]
        q, do = q_all[g, c, :, cols], do_all[g, c, :, cols]
        across = (((1,), (1,)), ((), ()))
        scores = lax.dot_general(keys, q, across, preferred_element_type=jnp.float32)
        prob_grad = lax.dot_general(values, do, across, preferred_element_type=jnp.float32)
        largest = jnp.max(scores, axis=0, keepdims=True)
        exponent = jnp.exp2((scores - largest) * power)
        prob = exponent * (1.0 / jnp.sum(exponent, axis=0, keepdims=True))
        prob_half = prob.astype(jnp.bfloat16)
        delta = jnp.sum(prob * prob_grad, axis=0, keepdims=True)
        score_half = (prob * (prob_grad - delta)).astype(jnp.bfloat16)
        value_term = jnp.dot(prob_half, do, preferred_element_type=jnp.float32)
        key_term = jnp.dot(score_half, q, preferred_element_type=jnp.float32)
        dq_t = jnp.dot(keys.T, score_half, preferred_element_type=jnp.float32)
        dq_all[g, c, :, cols] = (dq_t * scale).astype(jnp.bfloat16).T
        if r == 0:
            key_acc[...] = key_term
            value_acc[...] = value_term
        else:
            key_acc[...] += key_term
            value_acc[...] += value_term

    def begin(c):
        for j in range(listed):
            block = kv_now[siblings[0, c, j]]
            k_rows[j * span : (j + 1) * span, :] = block[:, :HEAD]
            v_rows[j * span : (j + 1) * span, :] = block[:, HEAD:]

    def end(g, c):
        listed_grads[c * reach : (c + 1) * reach, :HEAD] = (key_acc[...] * scale).astype(jnp.bfloat16)
        listed_grads[c * reach : (c + 1) * reach, HEAD:] = value_acc[...].astype(jnp.bfloat16)
        cols = pl.ds(pl.multiple_of(g * q_block, HEAD), q_block)
        pltpu.make_async_copy(dq_all.at[g, c], dq_hbm.at[0, c, :, cols], store_sem.at[g, c]).start()

    def again_plane(g):
        summing.finish(g, halves)
        again.start_plane(g)

    def again_line(g):
        again.wait_plane(g)
        again.start_line(g)

    def weigh(g):
        again.wait_line(g)
        grads = halves[g].reshape(rows, 2 * HEAD)
        got = jnp.dot(hidden_t[...], grads, preferred_element_type=jnp.float32)
        product[g] = got.reshape(product.shape[1:])
        shares[g, me_dp] = product[g, me_dp]
        for i in range(1, n_dp):
            peer = lax.rem(me_dp + i, n_dp)
            remote(
                product.at[g, peer],
                shares.at[g, me_dp],
                {"dp": peer},
                share_send.at[g],
                share_recv.at[g],
            ).start()

    def turn(it, carry):
        working = it < groups

        def slot(step, lag):
            g = it - lag

            @pl.when(jnp.logical_and(g >= 0, g < groups))
            def _():
                step(g)

        def run(c, chosen):
            @pl.when(working)
            def _():
                if 0 in chosen:
                    if c == 0:
                        first.wait_line(it)
                        kv_now[...] = kv[it].reshape(kv_now.shape)
                    begin(c)
                for r in chosen:
                    attend(it, c, r)
                if heads - 1 in chosen:
                    end(it, c)

        run(0, range(0, 2 * heads // 5))
        slot(again_line, 3)
        run(0, range(2 * heads // 5, heads))
        slot(again_plane, 2)
        run(1, range(0, 3 * heads // 5))
        slot(summing.line_to_plane, 1)
        run(1, range(3 * heads // 5, heads))

        @pl.when(working)
        def _():
            got = jnp.dot(placing[...], listed_grads[...], preferred_element_type=jnp.float32)
            part[it] = got.astype(jnp.bfloat16).reshape(part.shape[1:])
            summing.start_line(it)

        @pl.when(it == 2)
        def _():
            wait_blocks(hidden, n_seq - 1, summary_recv.at[0])
            hidden_t[...] = hidden[...].reshape(rows, hidden.shape[2]).T

        slot(weigh, 3)
        return carry

    lax.fori_loop(0, groups + 3, turn, 0)
    half = out_ref.shape[1] // 2
    for g in range(groups):
        wait_blocks(shares.at[g], n_dp - 1, share_recv.at[g])
        result = shares[g, 0]
        for d in range(1, n_dp):
            result = result + shares[g, d]
        out_ref[:, g * HEAD : (g + 1) * HEAD] = result[:, :HEAD]
        out_ref[:, half + g * HEAD : half + (g + 1) * HEAD] = result[:, HEAD:]

    def drain(g):
        first.wait_sent(g)
        again.wait_sent(g)
        summing.wait_sent(g)
        wait_blocks(shares.at[g], n_dp - 1, share_send.at[g])
        for c in range(own):
            pltpu.make_async_copy(
                dq_all.at[g, c], dq_hbm.at[0, c, :, pl.ds(0, q_block)], store_sem.at[g, c]
            ).wait()

    over_groups(drain)
    wait_blocks(hidden, n_seq - 1, summary_send.at[0])


def per_device(n_dp, n_seq, siblings, queries, grad_out, keys_in, input_values, summary):
    _, own, tokens, q_width = queries.shape
    span, kv_width = keys_in.shape[2], keys_in.shape[3]
    listed = siblings.shape[2]
    groups = kv_width // HEAD
    q_block = q_width // groups
    rows = own * span
    everyone = n_seq * rows
    block = summary.shape[3] // (n_dp * n_seq)
    any_space = pl.BlockSpec(memory_space=pl.ANY)
    vmem = pl.BlockSpec(memory_space=pltpu.VMEM)
    smem = pl.BlockSpec(memory_space=pltpu.SMEM)
    pieces = (
        summary.reshape(rows, n_dp, n_seq, block)
        .transpose(2, 0, 1, 3)
        .reshape(n_seq, rows, n_dp * block)
    )
    half = jnp.bfloat16
    tile = (span, 2 * HEAD)
    whole = pltpu.VMEM((groups, RING, 2, RING, own, *tile), half)
    tokens_all = pltpu.VMEM((groups, own, tokens, q_block), half)
    shares = pltpu.VMEM((groups, n_dp, block, 2 * HEAD), jnp.float32)
    pairs = pltpu.SemaphoreType.DMA((groups, 2))
    return pl.pallas_call(
        functools.partial(kernel, n_seq, n_dp),
        out_shape=(
            jax.ShapeDtypeStruct(queries.shape, half),
            jax.ShapeDtypeStruct((block, 2 * kv_width), jnp.float32),
        ),
        in_specs=[smem, vmem, vmem, vmem, any_space, any_space],
        out_specs=(any_space, vmem),
        scratch_shapes=[
            tokens_all,
            tokens_all,
            tokens_all,
            whole,
            pltpu.VMEM((n_seq * own, *tile), half),
            pltpu.VMEM((listed * span, HEAD), half),
            pltpu.VMEM((listed * span, HEAD), half),
            pltpu.VMEM((listed * span, HEAD), jnp.float32),
            pltpu.VMEM((listed * span, HEAD), jnp.float32),
            pltpu.VMEM((own * listed * span, 2 * HEAD), half),
            pltpu.VMEM((everyone, own * listed * span), half),
            whole,
            pltpu.VMEM((groups, RING - 1, 2, RING, *tile), half),
            pltpu.VMEM((groups, RING - 1, RING, 2, *tile), half),
            pltpu.VMEM((groups, 2, RING, *tile), half),
            pltpu.VMEM((groups, RING, 2, *tile), half),
            pltpu.VMEM((groups, 2, PLANE - 1, *tile), half),
            whole,
            pltpu.VMEM((n_seq, rows, n_dp * block), half),
            pltpu.VMEM((n_dp * block, everyone), half),
            shares,
            shares,
            pltpu.VMEM((2 * (RING - 1) * PLANE, *tile), half),
            pltpu.SemaphoreType.DMA((2, groups, own)),
            pltpu.SemaphoreType.DMA((groups, own)),
            *[pairs] * 6,
            pltpu.SemaphoreType.DMA((groups,)),
            pltpu.SemaphoreType.DMA((groups,)),
            pltpu.SemaphoreType.DMA((1,)),
            pltpu.SemaphoreType.DMA((1,)),
        ],
        compiler_params=pltpu.CompilerParams(
            collective_id=0, has_side_effects=True, vmem_limit_bytes=LIMIT
        ),
    )(siblings, keys_in[0], input_values[0], pieces, queries, grad_out)


def solution(mesh):
    placed = (
        P("dp", "seq", None),
        P("dp", "seq", None, None),
        P("dp", "seq", None, None),
        P("dp", "seq", None, None),
        P("dp", "seq", None, None),
        P("dp", "seq", None, None),
    )
    return jax.shard_map(
        functools.partial(per_device, mesh.shape["dp"], mesh.shape["seq"]),
        mesh=mesh,
        in_specs=placed,
        out_specs=(P("dp", "seq", None, None), P(("dp", "seq"), None)),
        check_vma=False,
    )
```

time: 1170 us -> 93.1 us (0.08)
  waiting for transfers between devices: 810 us -> 0 us
  blocking collectives: 186 us -> 0 us
  Pallas kernels: 0 us -> 81.5 us
  matrix products: 69.4 us -> 0 us
  local copies, waits for them, and re-layouts: 72.6 us -> 10.7 us
  other arithmetic: 18.8 us -> 0 us
  between operations: 14.8 us -> 0.66 us
    unnamed x4 -> x0, waiting for transfers between devices: 703 us -> none
    unnamed x1 -> x0, blocking collectives: 186 us -> none
    all_gather x2 -> x0, waiting for transfers between devices: 107 us -> none  [the longest x1 63.8 us: per_device(): lax.all_gather(keys_in, 'seq', axis=1, tiled=True)]
    pallas_call x0 -> x1, Pallas kernels: none -> 81.5 us  [per_device(): pl.pallas_call(functools.partial(kernel, n_seq, n_dp), out_shape=(jax.Sha...]
    dot_general x23 -> x0, matrix products: 47.6 us -> none  [the longest x4 8.75 us: group_grads(): jnp.einsum('ctrd,cld->crtl', incoming_gradient, value_tile_block, preferr...]
    unnamed x94 -> x4, local copies, waits for them, and re-layouts: 42.5 us -> 5.89 us
    sub x4 -> x0, matrix products: 21.8 us -> none  [group_grads(): exponent = jnp.exp(scores - largest)]
    convert_element_type x4 -> x0, other arithmetic: 13.4 us -> none  [group_grads(): prob_half = probability.astype(jnp.bfloat16)]
  transfers between devices with their start and end apart: 3 -> 0, of which waited for: 3 -> 0; matrix products, arithmetic and copies ran while one was open for 4% -> 0% of each run, Pallas kernels for 0% -> 0%
where the time goes in v3:
time: 93.1 us; the launch traced here: 92.9 us
  Pallas kernels  81.5 us (88%)
  local copies, waits for them, and re-layouts  10.7 us (11%)
    pallas_call x1, Pallas kernels, per_device(): pl.pallas_call(functools.partial(kernel, n_seq, n_dp), out_shape=(jax.Sha...  81.5 us
    unnamed x4, local copies, waits for them, and re-layouts  5.89 us
    reshape x2, local copies, waits for them, and re-layouts, per_device(): summary.reshape(rows, n_dp, n_seq, block).transpose(2, 0, 1, 3)  3.46 us

profile of v3, /device:TPU:1, one launch (start us, length us, event | category | flops | bytes accessed | tf_op | source)
XLA Modules:
  0.0 92.9 jit_solution(7111979714324157076)
XLA Ops:
  0.6 2.9 %reshape.10 = bf16[32,4,32,40]{3,2,1,0:T(8,128)(2,1)S(1)} reshape(bf16[1,2,16,5120]{3,2,1,0:T(8,128)(2,1)} %param.11) | data formatting | bytes 655360 | tf_op jit(solution)/shard_map/reshape | solution.py:416
  3.6 0.5 copy.10
  4.1 1.4 %reshape.11.s_ref = bf16[32,32,160]{2,1,0:T(8,128)(2,1)} reshape(bf16[32,32,4,40]{3,2,1,0:T(4,128)(2,1)S(1)} %bitcast.7) | data formatting | bytes 655360 | tf_op jit(solution)/shard_map/reshape | solution.py:418
  5.5 81.5 %shard_map.77 = (bf16[1,2,512,2560]{3,2,1,0:T(8,128)(2,1)}, f32[40,1024]{1,0:T(8,128)}) custom-call(s32[1,2,16]{2,1,0:T(2,128)} %siblings.1, bf16[2,16,512]{2,1,0:T(8,128)(2,1)} %bitcast.8, bf16[2,16,512]{2,1,0:T(8,128)(2,1)} %bitcast.9, bf16[32,32,160]{2,1,0:T(8,128)(2,1)} %reshape.11.s_ref, bf16[1,2,512,2560]{3,2,1,0:T(8,128)(2,1)} %q_hbm.1, ...), custom_call_target="tpu_custom_call" | custom-call | tf_op jit(solution)/shard_map/pallas_call | solution.py:426
  87.0 0.0 copy-start
  87.0 5.2 %copy.13 = bf16[1,2,512,2560]{3,2,1,0:T(8,128)(2,1)} copy(bf16[1,2,512,2560]{3,2,1,0:T(8,128)(2,1)} %get-tuple-element.4) | data formatting | bytes 10485760
  92.3 0.0 copy-done
  92.3 0.7 copy.14
Async XLA Ops:
  87.0 5.2 %copy-start = (f32[40,1024]{1,0:T(8,128)S(1)}, f32[40,1024]{1,0:T(8,128)}, u32[]{:S(2)}) copy-start(f32[40,1024]{1,0:T(8,128)} %get-tuple-element.5) | copy-start | bytes 491524

commit v4 on v3

--- a/solution.py
+++ b/solution.py
@@ -12,6 +12,7 @@
 MESH = pl.DeviceIdType.MESH
 LIMIT = 56 * 1024 * 1024
 RING = 4
+PART = 256
 PLANE = 2 * RING
 
 
@@ -184,6 +185,7 @@
     sum_b,
     plane,
     halves,
+    pieces,
     hidden,
     hidden_t,
     product,
@@ -258,42 +260,75 @@
 
     over_groups(line)
 
-    hidden[me] = s_ref[me]
+    block = pieces.shape[2] // n_dp
+    step = n_seq * block
+    for p in range(n_seq):
+        for c in range(own):
+            cut = [
+                s_ref[c, :, d * step + p * block : d * step + (p + 1) * block] for d in range(n_dp)
+            ]
+            pieces[p, c * span : (c + 1) * span, :] = jnp.concatenate(cut, axis=1)
+    hidden[me] = pieces[me]
 
     def push_summary(i, carry):
         peer = lax.rem(me + i, n_seq)
         remote(
-            s_ref.at[peer], hidden.at[me], {"seq": peer}, summary_send.at[0], summary_recv.at[0]
+            pieces.at[peer], hidden.at[me], {"seq": peer}, summary_send.at[0], summary_recv.at[0]
         ).start()
         return carry
 
-    lax.fori_loop(1, n_seq, push_summary, 0)
     for load in loads:
         load.wait()
 
-    def attend(g, c, r):
-        cols = slice(r * HEAD, (r + 1) * HEAD)
+    def attend(g, c):
         keys, values = k_rows[...], v_rows[...]
-        q, do = q_all[g, c, :, cols], do_all[g, c, :, cols]
+        keys_t = keys.T
+        size = min(PART, tokens)
+        parts = [(r, t) for r in range(heads) for t in range(0, tokens, size)]
         across = (((1,), (1,)), ((), ()))
-        scores = lax.dot_general(keys, q, across, preferred_element_type=jnp.float32)
-        prob_grad = lax.dot_general(values, do, across, preferred_element_type=jnp.float32)
-        largest = jnp.max(scores, axis=0, keepdims=True)
-        exponent = jnp.exp2((scores - largest) * power)
-        prob = exponent * (1.0 / jnp.sum(exponent, axis=0, keepdims=True))
-        prob_half = prob.astype(jnp.bfloat16)
-        delta = jnp.sum(prob * prob_grad, axis=0, keepdims=True)
-        score_half = (prob * (prob_grad - delta)).astype(jnp.bfloat16)
-        value_term = jnp.dot(prob_half, do, preferred_element_type=jnp.float32)
-        key_term = jnp.dot(score_half, q, preferred_element_type=jnp.float32)
-        dq_t = jnp.dot(keys.T, score_half, preferred_element_type=jnp.float32)
-        dq_all[g, c, :, cols] = (dq_t * scale).astype(jnp.bfloat16).T
-        if r == 0:
-            key_acc[...] = key_term
-            value_acc[...] = value_term
-        else:
-            key_acc[...] += key_term
-            value_acc[...] += value_term
+
+        def pick(ref, r, t):
+            return ref[g, c, t : t + size, r * HEAD : (r + 1) * HEAD]
+
+        def ahead(r, t):
+            return (
+                lax.dot_general(
+                    keys, pick(q_all, r, t), across, preferred_element_type=jnp.float32
+                ),
+                lax.dot_general(
+                    values, pick(do_all, r, t), across, preferred_element_type=jnp.float32
+                ),
+            )
+
+        def behind(r, t, prob_half, score_half):
+            value_term = jnp.dot(
+                prob_half, pick(do_all, r, t), preferred_element_type=jnp.float32
+            )
+            key_term = jnp.dot(score_half, pick(q_all, r, t), preferred_element_type=jnp.float32)
+            if (r, t) == (0, 0):
+                key_acc[...] = key_term
+                value_acc[...] = value_term
+            else:
+                key_acc[...] += key_term
+                value_acc[...] += value_term
+            dq_t = jnp.dot(keys_t, score_half, preferred_element_type=jnp.float32)
+            dq = (dq_t * scale).astype(jnp.bfloat16).T
+            dq_all[g, c, t : t + size, r * HEAD : (r + 1) * HEAD] = dq
+
+        coming, past = ahead(*parts[0]), None
+        for i, at in enumerate(parts):
+            scores, prob_grad = coming
+            if i + 1 < len(parts):
+                coming = ahead(*parts[i + 1])
+            if past is not None:
+                behind(*past)
+            largest = jnp.max(scores, axis=0, keepdims=True)
+            exponent = jnp.exp2((scores - largest) * power)
+            prob = exponent * (1.0 / jnp.sum(exponent, axis=0, keepdims=True))
+            delta = jnp.sum(prob * prob_grad, axis=0, keepdims=True)
+            score_half = (prob * (prob_grad - delta)).astype(jnp.bfloat16)
+            past = (*at, prob.astype(jnp.bfloat16), score_half)
+        behind(*past)
 
     def begin(c):
         for j in range(listed):
@@ -332,51 +367,43 @@
             ).start()
 
     def turn(it, carry):
-        working = it < groups
-
-        def slot(step, lag):
-            g = it - lag
-
-            @pl.when(jnp.logical_and(g >= 0, g < groups))
-            def _():
-                step(g)
-
-        def run(c, chosen):
-            @pl.when(working)
-            def _():
-                if 0 in chosen:
-                    if c == 0:
-                        first.wait_line(it)
-                        kv_now[...] = kv[it].reshape(kv_now.shape)
-                    begin(c)
-                for r in chosen:
-                    attend(it, c, r)
-                if heads - 1 in chosen:
-                    end(it, c)
-
-        run(0, range(0, 2 * heads // 5))
-        slot(again_line, 3)
-        run(0, range(2 * heads // 5, heads))
-        slot(again_plane, 2)
-        run(1, range(0, 3 * heads // 5))
-        slot(summing.line_to_plane, 1)
-        run(1, range(3 * heads // 5, heads))
-
-        @pl.when(working)
+        first.wait_line(it)
+        kv_now[...] = kv[it].reshape(kv_now.shape)
+        for c in range(own):
+            if c == own - 1:
+
+                @pl.when(it >= 2)
+                def _():
+                    summing.line_to_plane(it - 2)
+
+            begin(c)
+            attend(it, c)
+            end(it, c)
+        got = jnp.dot(placing[...], listed_grads[...], preferred_element_type=jnp.float32)
+        part[it] = got.astype(jnp.bfloat16).reshape(part.shape[1:])
+        summing.start_line(it)
+
+        @pl.when(it == 0)
         def _():
-            got = jnp.dot(placing[...], listed_grads[...], preferred_element_type=jnp.float32)
-            part[it] = got.astype(jnp.bfloat16).reshape(part.shape[1:])
-            summing.start_line(it)
-
-        @pl.when(it == 2)
-        def _():
-            wait_blocks(hidden, n_seq - 1, summary_recv.at[0])
-            hidden_t[...] = hidden[...].reshape(rows, hidden.shape[2]).T
-
-        slot(weigh, 3)
+            lax.fori_loop(1, n_seq, push_summary, 0)
+
         return carry
 
-    lax.fori_loop(0, groups + 3, turn, 0)
+    lax.fori_loop(0, groups, turn, 0)
+    wait_blocks(hidden, n_seq - 1, summary_recv.at[0])
+    hidden_t[...] = hidden[...].reshape(rows, hidden.shape[2]).T
+    for g in range(groups - 2):
+        again_plane(g)
+    for g in range(groups - 2, groups):
+        summing.line_to_plane(g)
+    for g in range(groups - 2):
+        again_line(g)
+    for g in range(groups - 2, groups):
+        again_plane(g)
+    for g in range(groups):
+        if g < 2:
+            again_line(groups - 2 + g)
+        weigh(g)
     half = out_ref.shape[1] // 2
     for g in range(groups):
         wait_blocks(shares.at[g], n_dp - 1, share_recv.at[g])
@@ -412,11 +439,6 @@
     any_space = pl.BlockSpec(memory_space=pl.ANY)
     vmem = pl.BlockSpec(memory_space=pltpu.VMEM)
     smem = pl.BlockSpec(memory_space=pltpu.SMEM)
-    pieces = (
-        summary.reshape(rows, n_dp, n_seq, block)
-        .transpose(2, 0, 1, 3)
-        .reshape(n_seq, rows, n_dp * block)
-    )
     half = jnp.bfloat16
     tile = (span, 2 * HEAD)
     whole = pltpu.VMEM((groups, RING, 2, RING, own, *tile), half)
@@ -451,6 +473,7 @@
             pltpu.VMEM((groups, 2, PLANE - 1, *tile), half),
             whole,
             pltpu.VMEM((n_seq, rows, n_dp * block), half),
+            pltpu.VMEM((n_seq, rows, n_dp * block), half),
             pltpu.VMEM((n_dp * block, everyone), half),
             shares,
             shares,
@@ -466,7 +489,7 @@
         compiler_params=pltpu.CompilerParams(
             collective_id=0, has_side_effects=True, vmem_limit_bytes=LIMIT
         ),
-    )(siblings, keys_in[0], input_values[0], pieces, queries, grad_out)
+    )(siblings, keys_in[0], input_values[0], summary[0], queries, grad_out)
 
 
 def solution(mesh):

time: 93.1 us -> 81.6 us (0.88)
  Pallas kernels: 81.5 us -> 75 us
  local copies, waits for them, and re-layouts: 10.7 us -> 5.89 us
    pallas_call x1, Pallas kernels: 81.5 us -> 75 us  [per_device(): pl.pallas_call(functools.partial(kernel, n_seq, n_dp), out_shape=(jax.Sha...]
    reshape x3 -> x0, local copies, waits for them, and re-layouts: 4.83 us -> none  [the longest x2 3.46 us: per_device(): summary.reshape(rows, n_dp, n_seq, block).transpose(2, 0, 1, 3)]
where the time goes in v4:
time: 81.6 us; the launch traced here: 81.5 us
  Pallas kernels  75 us (92%)
  local copies, waits for them, and re-layouts  5.89 us (7%)
    pallas_call x1, Pallas kernels, per_device(): pl.pallas_call(functools.partial(kernel, n_seq, n_dp), out_shape=(jax.Sha...  75 us
    unnamed x4, local copies, waits for them, and re-layouts  5.89 us

profile of v4, /device:TPU:1, one launch (start us, length us, event | category | flops | bytes accessed | tf_op | source)
XLA Modules:
  0.0 81.5 jit_solution(2045251662992574969)
XLA Ops:
  0.6 75.0 %shard_map.77 = (bf16[1,2,512,2560]{3,2,1,0:T(8,128)(2,1)}, f32[40,1024]{1,0:T(8,128)}) custom-call(s32[1,2,16]{2,1,0:T(2,128)} %siblings.1, bf16[2,16,512]{2,1,0:T(8,128)(2,1)} %bitcast.4, bf16[2,16,512]{2,1,0:T(8,128)(2,1)} %bitcast.5, bf16[2,16,5120]{2,1,0:T(8,128)(2,1)} %bitcast.3, bf16[1,2,512,2560]{3,2,1,0:T(8,128)(2,1)} %q_hbm.1, ...), custom_call_target="tpu_custom_call" | custom-call | tf_op jit(solution)/shard_map/pallas_call | solution.py:448
  75.6 0.0 copy-start
  75.6 5.2 %copy.10 = bf16[1,2,512,2560]{3,2,1,0:T(8,128)(2,1)} copy(bf16[1,2,512,2560]{3,2,1,0:T(8,128)(2,1)} %get-tuple-element.4) | data formatting | bytes 10485760
  80.8 0.0 copy-done
  80.8 0.7 copy.11
Async XLA Ops:
  75.6 5.2 %copy-start = (f32[40,1024]{1,0:T(8,128)S(1)}, f32[40,1024]{1,0:T(8,128)}, u32[]{:S(2)}) copy-start(f32[40,1024]{1,0:T(8,128)} %get-tuple-element.5) | copy-start | bytes 491524

commit v5 on v4

--- a/solution.py
+++ b/solution.py
@@ -100,6 +100,43 @@
     def wait_sent(self, g):
         wait_blocks(self.ruler, 2 * (PLANE - 1), self.send_sem.at[g, 0])
         wait_blocks(self.ruler, 2 * (RING - 1) * PLANE, self.send_sem.at[g, 1])
+
+
+class Halves:
+    def __init__(self, own, buf, ruler, send_sem, recv_sem):
+        self.own, self.buf, self.ruler = own, buf, ruler
+        self.send_sem, self.recv_sem = send_sem, recv_sem
+
+    def start_plane(self, g):
+        x, y, z = place()
+        self.buf[g, x, y, z] = self.own[g, y]
+        sems = (self.send_sem.at[g, 0], self.recv_sem.at[g, 0])
+        for dy, shift in plane_shifts():
+            other = lax.rem(y + dy, 2)
+            for half, peer in (
+                (0, peer_id(x, other, ring(z, shift))),
+                (1, peer_id(ring(x, shift), other, z)),
+            ):
+                remote(
+                    self.own.at[g, other, half], self.buf.at[g, x, y, z, half], peer, *sems
+                ).start()
+
+    def start_line(self, g):
+        x, y, z = place()
+        wait_blocks(self.ruler, PLANE - 1, self.recv_sem.at[g, 0])
+        sems = (self.send_sem.at[g, 1], self.recv_sem.at[g, 1])
+        for shift in (1, 3, 2):
+            first = self.buf.at[g, x, :, :, 0]
+            second = self.buf.at[g, :, :, z, 1]
+            remote(first, first, peer_id(ring(x, shift), y, z), *sems).start()
+            remote(second, second, peer_id(x, y, ring(z, shift)), *sems).start()
+
+    def wait_line(self, g):
+        wait_blocks(self.ruler, (RING - 1) * PLANE, self.recv_sem.at[g, 1])
+
+    def wait_sent(self, g):
+        wait_blocks(self.ruler, PLANE - 1, self.send_sem.at[g, 0])
+        wait_blocks(self.ruler, (RING - 1) * PLANE, self.send_sem.at[g, 1])
 
 
 class Reduce:
@@ -149,7 +186,9 @@
             total = wide(own)
             for i in range(PLANE - 1):
                 total += wide(self.plane[g, half, i])
-            out[g, x, y, z, half] = total.astype(out.dtype)
+            total = total.astype(jnp.bfloat16)
+            for which in range(2):
+                out.own[g, which, half] = total[:, which * HEAD : (which + 1) * HEAD]
 
     def wait_sent(self, g):
         wait_blocks(self.ruler, 2 * (RING - 1) * PLANE, self.send_sem.at[g, 0])
@@ -184,7 +223,8 @@
     sum_a,
     sum_b,
     plane,
-    halves,
+    sum_own,
+    sums,
     pieces,
     hidden,
     hidden_t,
@@ -217,7 +257,14 @@
 
     barrier = pltpu.get_barrier_semaphore()
     signal_peers(barrier, "seq", me, n_seq)
-    signal_peers(barrier, "dp", me_dp, n_dp)
+    for i in range(1, n_dp):
+        for across_y in range(2):
+            pl.semaphore_signal(
+                barrier,
+                inc=1,
+                device_id={"dp": lax.rem(me_dp + i, n_dp), **peer_id(x, across_y, z)},
+                device_id_type=MESH,
+            )
     loads = []
     for g in range(groups):
         cols = pl.ds(g * q_block, q_block)
@@ -230,10 +277,10 @@
         cols = slice(g * HEAD, (g + 1) * HEAD)
         kv[g, x, y, z, :, :, :HEAD] = k_ref[:, :, cols]
         kv[g, x, y, z, :, :, HEAD:] = v_ref[:, :, cols]
-    pl.semaphore_wait(barrier, n_seq + n_dp - 2)
+    pl.semaphore_wait(barrier, n_seq - 1 + 2 * (n_dp - 1))
 
     first = Spread(kv, ruler, spread_send, spread_recv)
-    again = Spread(halves, ruler, again_send, again_recv)
+    again = Halves(sum_own, sums, ruler, again_send, again_recv)
     summing = Reduce(part, line_a, line_b, sum_a, sum_b, plane, ruler, reduce_send, reduce_recv)
 
     def over_groups(step):
@@ -260,20 +307,28 @@
 
     over_groups(line)
 
-    block = pieces.shape[2] // n_dp
+    taken = pieces.shape[3] // own
+    block = taken // (2 * n_dp)
     step = n_seq * block
-    for p in range(n_seq):
-        for c in range(own):
-            cut = [
-                s_ref[c, :, d * step + p * block : d * step + (p + 1) * block] for d in range(n_dp)
+    for xs in range(RING):
+        for zs in range(RING):
+            starts = [
+                d * step + (xs * PLANE + ys * RING + zs) * block
+                for d in range(n_dp)
+                for ys in range(2)
             ]
-            pieces[p, c * span : (c + 1) * span, :] = jnp.concatenate(cut, axis=1)
-    hidden[me] = pieces[me]
+            cut = [s_ref[c, :, at : at + block] for c in range(own) for at in starts]
+            pieces[xs, zs] = jnp.concatenate(cut, axis=1)
+    hidden[me] = pieces[x, z]
 
     def push_summary(i, carry):
         peer = lax.rem(me + i, n_seq)
         remote(
-            pieces.at[peer], hidden.at[me], {"seq": peer}, summary_send.at[0], summary_recv.at[0]
+            pieces.at[peer // PLANE, lax.rem(peer, RING)],
+            hidden.at[me],
+            {"seq": peer},
+            summary_send.at[0],
+            summary_recv.at[0],
         ).start()
         return carry
 
@@ -343,25 +398,27 @@
         pltpu.make_async_copy(dq_all.at[g, c], dq_hbm.at[0, c, :, cols], store_sem.at[g, c]).start()
 
     def again_plane(g):
-        summing.finish(g, halves)
+        summing.finish(g, again)
         again.start_plane(g)
 
     def again_line(g):
-        again.wait_plane(g)
         again.start_line(g)
 
     def weigh(g):
         again.wait_line(g)
-        grads = halves[g].reshape(rows, 2 * HEAD)
-        got = jnp.dot(hidden_t[...], grads, preferred_element_type=jnp.float32)
+        got = 0.0
+        for c in range(own):
+            grads = sums[g, :, :, :, c].reshape(rows // own, HEAD)
+            got += jnp.dot(hidden_t[c], grads, preferred_element_type=jnp.float32)
         product[g] = got.reshape(product.shape[1:])
-        shares[g, me_dp] = product[g, me_dp]
-        for i in range(1, n_dp):
-            peer = lax.rem(me_dp + i, n_dp)
+        mine = me_dp * 2 + y
+        shares[g, mine] = product[g, mine]
+        for i in range(1, 2 * n_dp):
+            d, ys = lax.rem(me_dp + i // 2, n_dp), lax.rem(y + i % 2, 2)
             remote(
-                product.at[g, peer],
-                shares.at[g, me_dp],
-                {"dp": peer},
+                product.at[g, d * 2 + ys],
+                shares.at[g, mine],
+                {"dp": d, **peer_id(x, ys, z)},
                 share_send.at[g],
                 share_recv.at[g],
             ).start()
@@ -383,7 +440,7 @@
         part[it] = got.astype(jnp.bfloat16).reshape(part.shape[1:])
         summing.start_line(it)
 
-        @pl.when(it == 0)
+        @pl.when(it == 1)
         def _():
             lax.fori_loop(1, n_seq, push_summary, 0)
 
@@ -391,7 +448,9 @@
 
     lax.fori_loop(0, groups, turn, 0)
     wait_blocks(hidden, n_seq - 1, summary_recv.at[0])
-    hidden_t[...] = hidden[...].reshape(rows, hidden.shape[2]).T
+    for c in range(own):
+        columns = hidden[:, :, c * taken : (c + 1) * taken]
+        hidden_t[c] = columns.reshape(rows // own, taken).T
     for g in range(groups - 2):
         again_plane(g)
     for g in range(groups - 2, groups):
@@ -406,18 +465,18 @@
         weigh(g)
     half = out_ref.shape[1] // 2
     for g in range(groups):
-        wait_blocks(shares.at[g], n_dp - 1, share_recv.at[g])
-        result = shares[g, 0]
-        for d in range(1, n_dp):
-            result = result + shares[g, d]
-        out_ref[:, g * HEAD : (g + 1) * HEAD] = result[:, :HEAD]
-        out_ref[:, half + g * HEAD : half + (g + 1) * HEAD] = result[:, HEAD:]
+        wait_blocks(shares.at[g], 2 * n_dp - 1, share_recv.at[g])
+        for ys in range(2):
+            result = shares[g, ys]
+            for d in range(1, n_dp):
+                result = result + shares[g, 2 * d + ys]
+            out_ref[:, ys * half + g * HEAD : ys * half + (g + 1) * HEAD] = result
 
     def drain(g):
         first.wait_sent(g)
         again.wait_sent(g)
         summing.wait_sent(g)
-        wait_blocks(shares.at[g], n_dp - 1, share_send.at[g])
+        wait_blocks(shares.at[g], 2 * n_dp - 1, share_send.at[g])
         for c in range(own):
             pltpu.make_async_copy(
                 dq_all.at[g, c], dq_hbm.at[0, c, :, pl.ds(0, q_block)], store_sem.at[g, c]
@@ -440,10 +499,11 @@
     vmem = pl.BlockSpec(memory_space=pltpu.VMEM)
     smem = pl.BlockSpec(memory_space=pltpu.SMEM)
     half = jnp.bfloat16
-    tile = (span, 2 * HEAD)
+    tile, thin = (span, 2 * HEAD), (span, HEAD)
+    taken = 2 * n_dp * block
     whole = pltpu.VMEM((groups, RING, 2, RING, own, *tile), half)
     tokens_all = pltpu.VMEM((groups, own, tokens, q_block), half)
-    shares = pltpu.VMEM((groups, n_dp, block, 2 * HEAD), jnp.float32)
+    shares = pltpu.VMEM((groups, 2 * n_dp, block, HEAD), jnp.float32)
     pairs = pltpu.SemaphoreType.DMA((groups, 2))
     return pl.pallas_call(
         functools.partial(kernel, n_seq, n_dp),
@@ -471,10 +531,11 @@
             pltpu.VMEM((groups, 2, RING, *tile), half),
             pltpu.VMEM((groups, RING, 2, *tile), half),
             pltpu.VMEM((groups, 2, PLANE - 1, *tile), half),
-            whole,
-            pltpu.VMEM((n_seq, rows, n_dp * block), half),
-            pltpu.VMEM((n_seq, rows, n_dp * block), half),
-            pltpu.VMEM((n_dp * block, everyone), half),
+            pltpu.VMEM((groups, 2, own, *thin), half),
+            pltpu.VMEM((groups, RING, 2, RING, own, *thin), half),
+            pltpu.VMEM((RING, RING, span, own * taken), half),
+            pltpu.VMEM((n_seq, span, own * taken), half),
+            pltpu.VMEM((own, taken, everyone // own), half),
             shares,
             shares,
             pltpu.VMEM((2 * (RING - 1) * PLANE, *tile), half),

time: 81.6 us -> 79 us (0.968)
  Pallas kernels: 75 us -> 72.3 us
    pallas_call x1, Pallas kernels: 75 us -> 72.3 us  [per_device(): pl.pallas_call(functools.partial(kernel, n_seq, n_dp), out_shape=(jax.Sha...]
where the time goes in v5:
time: 79 us; the launch traced here: 78.9 us
  Pallas kernels  72.3 us (92%)
  local copies, waits for them, and re-layouts  5.89 us (7%)
    pallas_call x1, Pallas kernels, per_device(): pl.pallas_call(functools.partial(kernel, n_seq, n_dp), out_shape=(jax.Sha...  72.3 us
    unnamed x4, local copies, waits for them, and re-layouts  5.89 us

profile of v5, /device:TPU:1, one launch (start us, length us, event | category | flops | bytes accessed | tf_op | source)
XLA Modules:
  0.0 78.9 jit_solution(3358610567033533485)
XLA Ops:
  0.6 72.3 %shard_map.77 = (bf16[1,2,512,2560]{3,2,1,0:T(8,128)(2,1)}, f32[40,1024]{1,0:T(8,128)}) custom-call(s32[1,2,16]{2,1,0:T(2,128)} %siblings.1, bf16[2,16,512]{2,1,0:T(8,128)(2,1)} %bitcast.4, bf16[2,16,512]{2,1,0:T(8,128)(2,1)} %bitcast.5, bf16[2,16,5120]{2,1,0:T(8,128)(2,1)} %bitcast.3, bf16[1,2,512,2560]{3,2,1,0:T(8,128)(2,1)} %q_hbm.1, ...), custom_call_target="tpu_custom_call" | custom-call | tf_op jit(solution)/shard_map/pallas_call | solution.py:508
  73.0 0.0 copy-start
  73.0 5.2 %copy.10 = bf16[1,2,512,2560]{3,2,1,0:T(8,128)(2,1)} copy(bf16[1,2,512,2560]{3,2,1,0:T(8,128)(2,1)} %get-tuple-element.4) | data formatting | bytes 10485760
  78.2 0.0 copy-done
  78.2 0.7 copy.11
Async XLA Ops:
  73.0 5.2 %copy-start = (f32[40,1024]{1,0:T(8,128)S(1)}, f32[40,1024]{1,0:T(8,128)}, u32[]{:S(2)}) copy-start(f32[40,1024]{1,0:T(8,128)} %get-tuple-element.5) | copy-start | bytes 491524

commit v6 on v5

--- a/solution.py
+++ b/solution.py
@@ -63,7 +63,7 @@
 
 
 def plane_shifts():
-    return [(i // RING, i % RING) for i in range(1, PLANE)]
+    return [(1, 2), (1, 1), (1, 3), (0, 2), (1, 0), (0, 1), (0, 3)]
 
 
 class Spread:
@@ -87,7 +87,7 @@
 
     def start_line(self, g):
         x, y, z = place()
-        for shift in (1, 3, 2):
+        for shift in (2, 1, 3):
             first = self.buf.at[g, x, :, :, 0]
             second = self.buf.at[g, :, :, z, 1]
             sems = (self.send_sem.at[g, 1], self.recv_sem.at[g, 1])
@@ -125,7 +125,7 @@
         x, y, z = place()
         wait_blocks(self.ruler, PLANE - 1, self.recv_sem.at[g, 0])
         sems = (self.send_sem.at[g, 1], self.recv_sem.at[g, 1])
-        for shift in (1, 3, 2):
+        for shift in (2, 1, 3):
             first = self.buf.at[g, x, :, :, 0]
             second = self.buf.at[g, :, :, z, 1]
             remote(first, first, peer_id(ring(x, shift), y, z), *sems).start()
@@ -149,7 +149,7 @@
     def start_line(self, g):
         x, y, z = place()
         sems = (self.send_sem.at[g, 0], self.recv_sem.at[g, 0])
-        for shift in (1, 3, 2):
+        for shift in (2, 1, 3):
             xs, zs = ring(x, shift), ring(z, shift)
             slot = shift - 1
             remote(

time: 79 us -> 78 us (0.987)
  Pallas kernels: 72.3 us -> 71.4 us
    pallas_call x1, Pallas kernels: 72.3 us -> 71.4 us  [per_device(): pl.pallas_call(functools.partial(kernel, n_seq, n_dp), out_shape=(jax.Sha...]
where the time goes in v6:
time: 78 us; the launch traced here: 77.9 us
  Pallas kernels  71.4 us (92%)
  local copies, waits for them, and re-layouts  5.89 us (8%)
    pallas_call x1, Pallas kernels, per_device(): pl.pallas_call(functools.partial(kernel, n_seq, n_dp), out_shape=(jax.Sha...  71.4 us
    unnamed x4, local copies, waits for them, and re-layouts  5.89 us

profile of v6, /device:TPU:1, one launch (start us, length us, event | category | flops | bytes accessed | tf_op | source)
XLA Modules:
  0.0 77.9 jit_solution(16784423369454931112)
XLA Ops:
  0.6 71.4 %shard_map.77 = (bf16[1,2,512,2560]{3,2,1,0:T(8,128)(2,1)}, f32[40,1024]{1,0:T(8,128)}) custom-call(s32[1,2,16]{2,1,0:T(2,128)} %siblings.1, bf16[2,16,512]{2,1,0:T(8,128)(2,1)} %bitcast.4, bf16[2,16,512]{2,1,0:T(8,128)(2,1)} %bitcast.5, bf16[2,16,5120]{2,1,0:T(8,128)(2,1)} %bitcast.3, bf16[1,2,512,2560]{3,2,1,0:T(8,128)(2,1)} %q_hbm.1, ...), custom_call_target="tpu_custom_call" | custom-call | tf_op jit(solution)/shard_map/pallas_call | solution.py:508
  72.0 0.0 copy-start
  72.0 5.2 %copy.10 = bf16[1,2,512,2560]{3,2,1,0:T(8,128)(2,1)} copy(bf16[1,2,512,2560]{3,2,1,0:T(8,128)(2,1)} %get-tuple-element.4) | data formatting | bytes 10485760
  77.3 0.0 copy-done
  77.3 0.7 copy.11
Async XLA Ops:
  72.0 5.2 %copy-start = (f32[40,1024]{1,0:T(8,128)S(1)}, f32[40,1024]{1,0:T(8,128)}, u32[]{:S(2)}) copy-start(f32[40,1024]{1,0:T(8,128)} %get-tuple-element.5) | copy-start | bytes 491524

commit v7 on v6

--- a/solution.py
+++ b/solution.py
@@ -213,6 +213,7 @@
     kv_now,
     k_rows,
     v_rows,
+    score_all,
     key_acc,
     value_acc,
     listed_grads,
@@ -332,12 +333,9 @@
         ).start()
         return carry
 
-    for load in loads:
-        load.wait()
 
     def attend(g, c):
-        keys, values = k_rows[...], v_rows[...]
-        keys_t = keys.T
+        keys, values = k_rows[g, c], v_rows[...]
         size = min(PART, tokens)
         parts = [(r, t) for r in range(heads) for t in range(0, tokens, size)]
         across = (((1,), (1,)), ((), ()))
@@ -366,9 +364,7 @@
             else:
                 key_acc[...] += key_term
                 value_acc[...] += value_term
-            dq_t = jnp.dot(keys_t, score_half, preferred_element_type=jnp.float32)
-            dq = (dq_t * scale).astype(jnp.bfloat16).T
-            dq_all[g, c, t : t + size, r * HEAD : (r + 1) * HEAD] = dq
+            score_all[g, c, :, r * tokens + t : r * tokens + t + size] = score_half
 
         coming, past = ahead(*parts[0]), None
         for i, at in enumerate(parts):
@@ -385,17 +381,30 @@
             past = (*at, prob.astype(jnp.bfloat16), score_half)
         behind(*past)
 
-    def begin(c):
+    def begin(g, c):
         for j in range(listed):
             block = kv_now[siblings[0, c, j]]
-            k_rows[j * span : (j + 1) * span, :] = block[:, :HEAD]
+            k_rows[g, c, j * span : (j + 1) * span, :] = block[:, :HEAD]
             v_rows[j * span : (j + 1) * span, :] = block[:, HEAD:]
 
     def end(g, c):
         listed_grads[c * reach : (c + 1) * reach, :HEAD] = (key_acc[...] * scale).astype(jnp.bfloat16)
         listed_grads[c * reach : (c + 1) * reach, HEAD:] = value_acc[...].astype(jnp.bfloat16)
-        cols = pl.ds(pl.multiple_of(g * q_block, HEAD), q_block)
-        pltpu.make_async_copy(dq_all.at[g, c], dq_hbm.at[0, c, :, cols], store_sem.at[g, c]).start()
+
+    def query_gradient(g):
+        def one(c, carry):
+            keys_t = k_rows[g, c].T
+            for r in range(heads):
+                scores = score_all[g, c, :, r * tokens : (r + 1) * tokens]
+                dq_t = jnp.dot(keys_t, scores, preferred_element_type=jnp.float32)
+                dq_all[g, c, :, r * HEAD : (r + 1) * HEAD] = (dq_t * scale).astype(jnp.bfloat16).T
+            cols = pl.ds(g * q_block, q_block)
+            pltpu.make_async_copy(
+                dq_all.at[g, c], dq_hbm.at[0, c, :, cols], store_sem.at[g, c]
+            ).start()
+            return carry
+
+        lax.fori_loop(0, own, one, 0)
 
     def again_plane(g):
         summing.finish(g, again)
@@ -433,7 +442,9 @@
                 def _():
                     summing.line_to_plane(it - 2)
 
-            begin(c)
+            begin(it, c)
+            for kind, ref in ((0, q_all), (1, do_all)):
+                pltpu.make_async_copy(ref.at[it, c], ref.at[it, c], load_sem.at[kind, it, c]).wait()
             attend(it, c)
             end(it, c)
         got = jnp.dot(placing[...], listed_grads[...], preferred_element_type=jnp.float32)
@@ -447,22 +458,29 @@
         return carry
 
     lax.fori_loop(0, groups, turn, 0)
+    last = groups - 1
+    for g in range(groups - 2):
+        again_plane(g)
+    summing.line_to_plane(last - 1)
+    query_gradient(0)
+    summing.line_to_plane(last)
+    for g in range(groups - 2):
+        again_line(g)
+    again_plane(last - 1)
     wait_blocks(hidden, n_seq - 1, summary_recv.at[0])
     for c in range(own):
         columns = hidden[:, :, c * taken : (c + 1) * taken]
         hidden_t[c] = columns.reshape(rows // own, taken).T
-    for g in range(groups - 2):
-        again_plane(g)
-    for g in range(groups - 2, groups):
-        summing.line_to_plane(g)
-    for g in range(groups - 2):
-        again_line(g)
-    for g in range(groups - 2, groups):
-        again_plane(g)
-    for g in range(groups):
-        if g < 2:
-            again_line(groups - 2 + g)
-        weigh(g)
+    query_gradient(1)
+    again_plane(last)
+    again_line(last - 1)
+    weigh(0)
+    query_gradient(last - 1)
+    again_line(last)
+    weigh(1)
+    weigh(last - 1)
+    query_gradient(last)
+    weigh(last)
     half = out_ref.shape[1] // 2
     for g in range(groups):
         wait_blocks(shares.at[g], 2 * n_dp - 1, share_recv.at[g])
@@ -492,6 +510,7 @@
     listed = siblings.shape[2]
     groups = kv_width // HEAD
     q_block = q_width // groups
+    heads = q_block // HEAD
     rows = own * span
     everyone = n_seq * rows
     block = summary.shape[3] // (n_dp * n_seq)
@@ -519,8 +538,9 @@
             tokens_all,
             whole,
             pltpu.VMEM((n_seq * own, *tile), half),
+            pltpu.VMEM((groups, own, listed * span, HEAD), half),
             pltpu.VMEM((listed * span, HEAD), half),
-            pltpu.VMEM((listed * span, HEAD), half),
+            pltpu.VMEM((groups, own, listed * span, heads * tokens), half),
             pltpu.VMEM((listed * span, HEAD), jnp.float32),
             pltpu.VMEM((listed * span, HEAD), jnp.float32),
             pltpu.VMEM((own * listed * span, 2 * HEAD), half),

time: 78 us -> 77.9 us (level)
  no operation moved by 1% of the time
where the time goes in v7:
time: 77.9 us; the launch traced here: 77.8 us
  Pallas kernels  71.2 us (91%)
  local copies, waits for them, and re-layouts  5.89 us (8%)
    pallas_call x1, Pallas kernels, per_device(): pl.pallas_call(functools.partial(kernel, n_seq, n_dp), out_shape=(jax.Sha...  71.2 us
    unnamed x4, local copies, waits for them, and re-layouts  5.89 us

profile of v7, /device:TPU:1, one launch (start us, length us, event | category | flops | bytes accessed | tf_op | source)
XLA Modules:
  0.0 77.8 jit_solution(1963027207625822007)
XLA Ops:
  0.6 71.2 %shard_map.77 = (bf16[1,2,512,2560]{3,2,1,0:T(8,128)(2,1)}, f32[40,1024]{1,0:T(8,128)}) custom-call(s32[1,2,16]{2,1,0:T(2,128)} %siblings.1, bf16[2,16,512]{2,1,0:T(8,128)(2,1)} %bitcast.4, bf16[2,16,512]{2,1,0:T(8,128)(2,1)} %bitcast.5, bf16[2,16,5120]{2,1,0:T(8,128)(2,1)} %bitcast.3, bf16[1,2,512,2560]{3,2,1,0:T(8,128)(2,1)} %q_hbm.1, ...), custom_call_target="tpu_custom_call" | custom-call | tf_op jit(solution)/shard_map/pallas_call | solution.py:527
  71.9 0.0 copy-start
  71.9 5.2 %copy.10 = bf16[1,2,512,2560]{3,2,1,0:T(8,128)(2,1)} copy(bf16[1,2,512,2560]{3,2,1,0:T(8,128)(2,1)} %get-tuple-element.4) | data formatting | bytes 10485760
  77.1 0.0 copy-done
  77.1 0.7 copy.11
Async XLA Ops:
  71.9 5.2 %copy-start = (f32[40,1024]{1,0:T(8,128)S(1)}, f32[40,1024]{1,0:T(8,128)}, u32[]{:S(2)}) copy-start(f32[40,1024]{1,0:T(8,128)} %get-tuple-element.5) | copy-start | bytes 491524
